TPU v7x, 128 devices: a whole 4x4x4 slice. The times are simulated.
128 devices in a mesh: ctx: 32 (over y, z, x_lo), head: 4 (over x_hi, core).
Axes of the slice: x: 4 (x_hi: 2, x_lo: 2; x = x_hi * 2 + x_lo), y: 4, z: 4, core: 2. Of those that a mesh axis runs over, the one named last changes fastest.
Arguments:
- x_in: bfloat16 [49152, 8192], P('ctx', 'head'), may hold values from -6 to 6
- b_in: bfloat16 [49152, 1024], P('ctx', 'head'), may hold values from -6 to 6
- c_in: bfloat16 [49152, 1024], P('ctx', 'head'), may hold values from -6 to 6
- conv_x: bfloat16 [4, 8192], P(None, 'head'), may hold values from -3 to 3
- conv_b: bfloat16 [4, 1024], P(None, 'head'), may hold values from -3 to 3
- conv_c: bfloat16 [4, 1024], P(None, 'head'), may hold values from -3 to 3
- step_size: float32 [49152, 128], P('ctx', 'head'), may hold values from 0.0022552745 to 13.30215
- decay_rate: float32 [128], P('head'), may hold values from 0.0011276372 to 8.313844
- skip: float32 [128], P('head'), may hold values from 0.5 to 2
- gate: bfloat16 [49152, 8192], P('ctx', 'head'), may hold values from -200 to 200
- norm_gain: bfloat16 [8192], P('head'), may hold values from 0.099609375 to 1.8984375
- doc_starts: int32 [4], replicated, may hold values from 0 to 49151, as said below
Outputs:
- mixed: bfloat16 [49152, 8192], P('ctx', 'head')
Inputs may be any that keep to these rules, and one draw needn't show every extreme that they name: `doc_starts`: strictly increasing; the first entry is 0 and the last is 49151, so the last document is the single final token.
All inputs are finite; a program needn't handle non-finite values.
Results may differ from a plain program's by a relative error of at most 0.0042.
Values may be sent and summed in bfloat16 or wider, within the bound.
A program may use at most 192 MiB of HBM per device.

v0:
```python
import jax
import jax.numpy as jnp
from jax import lax
from jax.sharding import PartitionSpec as P

H = 128
P_SIZE = 64
N = 128
K = 4
Q = 768


EPS = 1e-05


def passed_along(x, axis, by):
    devices = lax.axis_size(axis)
    pairs = [(i, i + by) for i in range(devices) if 0 <= i + by < devices]
    return lax.ppermute(x, axis, pairs)


def segment_ids(doc_starts, positions):
    return jnp.sum((positions[:, None] >= doc_starts[None, :]).astype(jnp.int32), axis=1) - 1


def conv_silu(padded, taps, seg_padded, row_count):
    seg_now = seg_padded[K - 1 :]
    summed = jnp.zeros((row_count, padded.shape[1]), jnp.float32)
    for tap_index in range(K):
        window = padded[tap_index : tap_index + row_count].astype(jnp.float32)
        keeper = (seg_padded[tap_index : tap_index + row_count] == seg_now)[:, None]
        summed = summed + jnp.where(
            keeper, window * taps[tap_index].astype(jnp.float32)[None, :], 0.0
        )
    return jax.nn.silu(summed).astype(jnp.bfloat16)


def block_terms(x_conv, b_conv, c_conv, step, rate, skip, segment, seg_before):
    row_count = x_conv.shape[0]
    head_count = step.shape[1]
    groups = b_conv.shape[1] // N
    per_group = head_count // groups
    x_heads = x_conv.reshape(row_count, groups, per_group, P_SIZE)
    b_groups = b_conv.reshape(row_count, groups, N)
    c_groups = c_conv.reshape(row_count, groups, N)
    log_decay = jnp.cumsum(-step * rate[None, :], axis=0)
    position = jnp.arange(row_count, dtype=jnp.int32)
    allowed = (position[:, None] >= position[None, :]) & (segment[:, None] == segment[None, :])
    pieces = []
    for group_index in range(groups):
        head_start = group_index * per_group
        cum_t = log_decay[:, head_start : head_start + per_group].T
        decays = jnp.where(
            allowed[None], jnp.exp(jnp.minimum(cum_t[:, :, None] - cum_t[:, None, :], 0.0)), 0.0
        )
        scores = jnp.einsum(
            "in,jn->ij",
            c_groups[:, group_index],
            b_groups[:, group_index],
            preferred_element_type=jnp.float32,
        )
        weights = (
            scores[None] * decays * step[:, head_start : head_start + per_group].T[:, None, :]
        ).astype(jnp.bfloat16)
        pieces.append(
            jnp.einsum(
                "kij,jkp->ikp", weights, x_heads[:, group_index], preferred_element_type=jnp.float32
            )
        )
    intra = jnp.stack(pieces, axis=1)
    last_row = row_count - 1
    end_weight = (
        jnp.where(
            (segment == segment[last_row])[:, None],
            jnp.exp(log_decay[last_row][None, :] - log_decay),
            0.0,
        )
        * step
    )
    weighted_b = (
        b_groups[:, :, None, :] * end_weight.reshape(row_count, groups, per_group)[:, :, :, None]
    ).astype(jnp.bfloat16)
    local_state = jnp.einsum(
        "jgkn,jgkp->gknp", weighted_b, x_heads, preferred_element_type=jnp.float32
    )
    carry = jnp.where(segment[last_row] == seg_before, jnp.exp(log_decay[last_row]), 0.0)
    inflow = jnp.where((segment == seg_before)[:, None], jnp.exp(log_decay), 0.0)
    part = intra + skip.reshape(1, groups, per_group, 1) * x_heads.astype(jnp.float32)
    return (part.reshape(row_count, -1), local_state, carry, inflow)


def cross_term(c_conv, state_in, inflow):
    row_count = c_conv.shape[0]
    groups = state_in.shape[0]
    c_groups = c_conv.reshape(row_count, groups, N).astype(jnp.float32)
    result = jnp.einsum("ign,gknp->igkp", c_groups, state_in, precision=lax.Precision.HIGHEST)
    return (result * inflow.reshape(row_count, groups, -1)[:, :, :, None]).reshape(row_count, -1)


def shards(
    x_in,
    b_in,
    c_in,
    conv_x,
    conv_b,
    conv_c,
    step_size,
    decay_rate,
    skip,
    gate,
    norm_gain,
    doc_starts,
):
    row_count = x_in.shape[0]
    rim_rows = K - 1
    block_count = row_count // Q
    positions = (
        lax.axis_index("ctx") * row_count
        - rim_rows
        + jnp.arange(row_count + rim_rows, dtype=jnp.int32)
    )
    seg_pad = segment_ids(doc_starts, positions)
    tail_rows = row_count - rim_rows
    x_rim, b_rim, c_rim = passed_along(
        (x_in[tail_rows:], b_in[tail_rows:], c_in[tail_rows:]), "ctx", 1
    )
    x_conv = conv_silu(jnp.concatenate([x_rim, x_in], axis=0), conv_x, seg_pad, row_count)
    b_conv = conv_silu(jnp.concatenate([b_rim, b_in], axis=0), conv_b, seg_pad, row_count)
    c_conv = conv_silu(jnp.concatenate([c_rim, c_in], axis=0), conv_c, seg_pad, row_count)
    seg_blocks = seg_pad[rim_rows:].reshape(block_count, Q)
    seg_firsts = seg_pad[rim_rows - 1 :: Q][:block_count]
    c_blocks = c_conv.reshape(block_count, Q, -1)

    def first_pass(items):
        x_block, b_block, c_block, step_block, seg_block, before_block = items
        return block_terms(
            x_block, b_block, c_block, step_block, decay_rate, skip, seg_block, before_block
        )

    parts, local_states, carries, inflows = lax.map(
        first_pass,
        (
            x_conv.reshape(block_count, Q, -1),
            b_conv.reshape(block_count, Q, -1),
            c_blocks,
            step_size.reshape(block_count, Q, -1),
            seg_blocks,
            seg_firsts,
        ),
    )
    groups = local_states.shape[1]
    per_group = local_states.shape[2]

    def fold_block(summary, items):
        carry_now, state_now = items
        factor_now = carry_now.reshape(groups, per_group)
        return (
            (summary[0] * factor_now, summary[1] * factor_now[:, :, None, None] + state_now),
            None,
        )

    start_summary = (
        jnp.ones((groups, per_group), jnp.float32),
        jnp.zeros(local_states.shape[1:], jnp.float32),
    )
    (dev_factor, dev_state), unused = lax.scan(fold_block, start_summary, (carries, local_states))
    flat_state = dev_state.reshape(groups, per_group, -1)

    def relay(turn_index, incoming):
        return passed_along(dev_factor[:, :, None] * incoming + flat_state, "ctx", 1)

    incoming = lax.fori_loop(0, lax.axis_size("ctx") - 1, relay, jnp.zeros_like(flat_state))
    incoming = incoming.reshape(dev_state.shape)

    def second_pass(state_in, items):
        c_block, inflow, carry_now, local_now, part_now, gate_now = items
        result = part_now + cross_term(c_block, state_in, inflow)
        gated = result * jax.nn.silu(gate_now.astype(jnp.float32))
        next_state = carry_now.reshape(groups, per_group)[:, :, None, None] * state_in + local_now
        return (next_state, (gated, jnp.sum(gated * gated, axis=1)))

    unused_state, (gated_all, squares) = lax.scan(
        second_pass,
        incoming,
        (c_blocks, inflows, carries, local_states, parts, gate.reshape(block_count, Q, -1)),
    )
    totals = lax.psum(squares.reshape(-1), "head")
    scaling = lax.rsqrt(totals / (H * P_SIZE) + EPS)
    return (
        gated_all.reshape(row_count, -1) * scaling[:, None] * norm_gain.astype(jnp.float32)[None, :]
    ).astype(jnp.bfloat16)


def solution(mesh):
    in_specs = (
        P("ctx", "head"),
        P("ctx", "head"),
        P("ctx", "head"),
        P(None, "head"),
        P(None, "head"),
        P(None, "head"),
        P("ctx", "head"),
        P("head"),
        P("head"),
        P("ctx", "head"),
        P("head"),
        P(),
    )
    out_specs = P("ctx", "head")
    return jax.shard_map(shards, mesh=mesh, in_specs=in_specs, out_specs=out_specs, check_vma=False)
```

profile of v0, /device:TPU:24, one launch (start us, length us, event | category | flops | bytes accessed | tf_op | source)
XLA Modules:
  0.0 1139.9 jit_solution(5823090605364333602)
XLA Ops:
  0.7 3.4 collective-permute-start.2
  4.9 3.8 collective-permute-start.1
  9.4 3.4 collective-permute-start.3
  20.5 4.5 multiply_convert_fusion.16
  25.0 5.1 multiply_convert_fusion.15
  31.3 18.1 %multiply_convert_fusion.14 = bf16[1536,2048]{1,0:T(8,128)(2,1)} fusion(bf16[1536,2048]{1,0:T(8,128)(2,1)} %param.20, bf16[3,2048]{1,0:T(4,128)(2,1)S(1)} %collective-permute-done.1, f32[2048]{0:T(1024)S(1)} %bitcast.273, f32[2048]{0:T(1024)S(1)} %bitcast.274, f32[2048]{0:T(1024)S(1)} %bitcast.272, f32[2048]{0:T(1024)S(1)} %bitcast.271, ...), kind=kLoop, calls=%fused_computation.82 | loop fusion | flops 88080384 | bytes 12632576 | tf_op jit(solution)/shard_map/convert_element_type | solution.py:35
  49.4 155.8 %while.53 = (s32[]{:T(128)}, f32[2,768,2048]{1,2,0:T(8,128)}, f32[2,2,16,128,64]{3,4,2,1,0:T(8,128)}, f32[2,32]{1,0:T(2,128)}, f32[2,768,32]{1,2,0:T(8,128)}, /*...) while((s32[]{:T(128)}, f32[2,768,2048]{1,2,0:T(8,128)}, ...), condition=%wide.region_4.5_spmd, body=%wide.region_1.4_spmd.sunk | while | flops 3251505664 | bytes 92436528 | solution.py:140
  80.0 14.3 %fusion.59 = f32[768,1,16,64]{0,3,2,1:T(8,128)S(1)} fusion(f32[16,768]{1,0:T(8,128)} %get-tuple-element.580, f32[16,768]{1,0:T(8,128)} %get-tuple-element.581, f32[768,768]{1,0:T(8,128)} %fusion.58, pred[768,768]{1,0:T(8,128)(4,1)S(1)} %fusion.56, bf16[768,2,16,64]{0,3,2,1:T(8,128)(2,1)} %bitcast.251), kind=kOutput, calls=%fused_computation.16.clone.1 | convolution fusion | flops 1264582656 | bytes 7815168 | tf_op jit(solution)/shard_map/while/body/eval_jaxpr/kij,jkp->ikp/dot_general | solution.py:66
  94.8 13.1 %fusion.57 = f32[768,1,16,64]{0,3,2,1:T(8,128)S(1)} fusion(f32[16,768]{1,0:T(8,128)S(1)} %copy-done.10, f32[16,768]{1,0:T(8,128)S(1)} %copy-done.11, f32[768,768]{1,0:T(8,128)S(1)} %fusion.55, pred[768,768]{1,0:T(8,128)(4,1)S(1)} %fusion.56, bf16[768,2,16,64]{0,3,2,1:T(8,128)(2,1)S(1)} %bitcast.252), kind=kOutput, calls=%fused_computation.15.clone.1 | convolution fusion | flops 1264582656 | bytes 7815168 | tf_op jit(solution)/shard_map/while/body/eval_jaxpr/kij,jkp->ikp/dot_general | solution.py:66
  112.6 6.1 add_dynamic-update-slice_fusion.2
  128.2 6.1 fusion.60
  150.1 14.3 %fusion.59 = f32[768,1,16,64]{0,3,2,1:T(8,128)S(1)} fusion(f32[16,768]{1,0:T(8,128)} %get-tuple-element.580, f32[16,768]{1,0:T(8,128)} %get-tuple-element.581, f32[768,768]{1,0:T(8,128)} %fusion.58, pred[768,768]{1,0:T(8,128)(4,1)S(1)} %fusion.56, bf16[768,2,16,64]{0,3,2,1:T(8,128)(2,1)} %bitcast.251), kind=kOutput, calls=%fused_computation.16.clone.1 | convolution fusion | flops 1264582656 | bytes 7815168 | tf_op jit(solution)/shard_map/while/body/eval_jaxpr/kij,jkp->ikp/dot_general | solution.py:66
  164.9 13.1 %fusion.57 = f32[768,1,16,64]{0,3,2,1:T(8,128)S(1)} fusion(f32[16,768]{1,0:T(8,128)S(1)} %copy-done.10, f32[16,768]{1,0:T(8,128)S(1)} %copy-done.11, f32[768,768]{1,0:T(8,128)S(1)} %fusion.55, pred[768,768]{1,0:T(8,128)(4,1)S(1)} %fusion.56, bf16[768,2,16,64]{0,3,2,1:T(8,128)(2,1)S(1)} %bitcast.252), kind=kOutput, calls=%fused_computation.15.clone.1 | convolution fusion | flops 1264582656 | bytes 7815168 | tf_op jit(solution)/shard_map/while/body/eval_jaxpr/kij,jkp->ikp/dot_general | solution.py:66
  182.7 6.1 add_dynamic-update-slice_fusion.2
  198.3 6.1 fusion.60
  205.2 11.3 while.56
  218.8 816.4 %while.54 = (s32[]{:T(128)}, f32[2,16,8192]{2,1,0:T(8,128)S(1)}, f32[2,16]{1,0:T(2,128)}, f32[2,16,8192]{2,1,0:T(8,128)S(1)}, s32[]{:T(128)}) while((s32[]{:T(128)}, f32[2,16,8192]{2,1,0:T(8,128)S(1)}, f32[2,16]{1,0:T(2,128)}, f32[2,16,8192]{2,1,0:T(8,128)S(1)}, s32[]{:T(128)}) %tuple.101), condition=%wide.region_8.9_spmd, body=%wide.region_7.8_spmd.sunk | while | flops 524290 | bytes 7340261 | solution.py:172
  219.6 3.8 collective-permute-start
  223.4 25.1 %collective-permute-done = f32[2,16,8192]{2,1,0:T(8,128)S(1)} collective-permute-done((f32[2,16,8192]{2,1,0:T(8,128)S(1)}, f32[2,16,8192]{2,1,0:T(8,128)S(1)}, u32[]{:S(2)}, u32[]{:S(2)}) %collective-permute-start) | collective-permute-done | bytes 1048608 | tf_op jit(solution)/shard_map/while/body/eval_jaxpr/ppermute | solution.py:19
  251.3 26.1 %collective-permute-done = f32[2,16,8192]{2,1,0:T(8,128)S(1)} collective-permute-done((f32[2,16,8192]{2,1,0:T(8,128)S(1)}, f32[2,16,8192]{2,1,0:T(8,128)S(1)}, u32[]{:S(2)}, u32[]{:S(2)}) %collective-permute-start) | collective-permute-done | bytes 1048608 | tf_op jit(solution)/shard_map/while/body/eval_jaxpr/ppermute | solution.py:19
  280.2 25.2 %collective-permute-done = f32[2,16,8192]{2,1,0:T(8,128)S(1)} collective-permute-done((f32[2,16,8192]{2,1,0:T(8,128)S(1)}, f32[2,16,8192]{2,1,0:T(8,128)S(1)}, u32[]{:S(2)}, u32[]{:S(2)}) %collective-permute-start) | collective-permute-done | bytes 1048608 | tf_op jit(solution)/shard_map/while/body/eval_jaxpr/ppermute | solution.py:19
  308.1 24.3 %collective-permute-done = f32[2,16,8192]{2,1,0:T(8,128)S(1)} collective-permute-done((f32[2,16,8192]{2,1,0:T(8,128)S(1)}, f32[2,16,8192]{2,1,0:T(8,128)S(1)}, u32[]{:S(2)}, u32[]{:S(2)}) %collective-permute-start) | collective-permute-done | bytes 1048608 | tf_op jit(solution)/shard_map/while/body/eval_jaxpr/ppermute | solution.py:19
  335.2 23.3 %collective-permute-done = f32[2,16,8192]{2,1,0:T(8,128)S(1)} collective-permute-done((f32[2,16,8192]{2,1,0:T(8,128)S(1)}, f32[2,16,8192]{2,1,0:T(8,128)S(1)}, u32[]{:S(2)}, u32[]{:S(2)}) %collective-permute-start) | collective-permute-done | bytes 1048608 | tf_op jit(solution)/shard_map/while/body/eval_jaxpr/ppermute | solution.py:19
  361.3 22.4 %collective-permute-done = f32[2,16,8192]{2,1,0:T(8,128)S(1)} collective-permute-done((f32[2,16,8192]{2,1,0:T(8,128)S(1)}, f32[2,16,8192]{2,1,0:T(8,128)S(1)}, u32[]{:S(2)}, u32[]{:S(2)}) %collective-permute-start) | collective-permute-done | bytes 1048608 | tf_op jit(solution)/shard_map/while/body/eval_jaxpr/ppermute | solution.py:19
  386.5 21.5 %collective-permute-done = f32[2,16,8192]{2,1,0:T(8,128)S(1)} collective-permute-done((f32[2,16,8192]{2,1,0:T(8,128)S(1)}, f32[2,16,8192]{2,1,0:T(8,128)S(1)}, u32[]{:S(2)}, u32[]{:S(2)}) %collective-permute-start) | collective-permute-done | bytes 1048608 | tf_op jit(solution)/shard_map/while/body/eval_jaxpr/ppermute | solution.py:19
  410.7 20.6 %collective-permute-done = f32[2,16,8192]{2,1,0:T(8,128)S(1)} collective-permute-done((f32[2,16,8192]{2,1,0:T(8,128)S(1)}, f32[2,16,8192]{2,1,0:T(8,128)S(1)}, u32[]{:S(2)}, u32[]{:S(2)}) %collective-permute-start) | collective-permute-done | bytes 1048608 | tf_op jit(solution)/shard_map/while/body/eval_jaxpr/ppermute | solution.py:19
  434.1 20.6 %collective-permute-done = f32[2,16,8192]{2,1,0:T(8,128)S(1)} collective-permute-done((f32[2,16,8192]{2,1,0:T(8,128)S(1)}, f32[2,16,8192]{2,1,0:T(8,128)S(1)}, u32[]{:S(2)}, u32[]{:S(2)}) %collective-permute-start) | collective-permute-done | bytes 1048608 | tf_op jit(solution)/shard_map/while/body/eval_jaxpr/ppermute | solution.py:19
  457.4 20.6 %collective-permute-done = f32[2,16,8192]{2,1,0:T(8,128)S(1)} collective-permute-done((f32[2,16,8192]{2,1,0:T(8,128)S(1)}, f32[2,16,8192]{2,1,0:T(8,128)S(1)}, u32[]{:S(2)}, u32[]{:S(2)}) %collective-permute-start) | collective-permute-done | bytes 1048608 | tf_op jit(solution)/shard_map/while/body/eval_jaxpr/ppermute | solution.py:19
  480.7 20.6 %collective-permute-done = f32[2,16,8192]{2,1,0:T(8,128)S(1)} collective-permute-done((f32[2,16,8192]{2,1,0:T(8,128)S(1)}, f32[2,16,8192]{2,1,0:T(8,128)S(1)}, u32[]{:S(2)}, u32[]{:S(2)}) %collective-permute-start) | collective-permute-done | bytes 1048608 | tf_op jit(solution)/shard_map/while/body/eval_jaxpr/ppermute | solution.py:19
  504.0 21.4 %collective-permute-done = f32[2,16,8192]{2,1,0:T(8,128)S(1)} collective-permute-done((f32[2,16,8192]{2,1,0:T(8,128)S(1)}, f32[2,16,8192]{2,1,0:T(8,128)S(1)}, u32[]{:S(2)}, u32[]{:S(2)}) %collective-permute-start) | collective-permute-done | bytes 1048608 | tf_op jit(solution)/shard_map/while/body/eval_jaxpr/ppermute | solution.py:19
  528.2 22.5 %collective-permute-done = f32[2,16,8192]{2,1,0:T(8,128)S(1)} collective-permute-done((f32[2,16,8192]{2,1,0:T(8,128)S(1)}, f32[2,16,8192]{2,1,0:T(8,128)S(1)}, u32[]{:S(2)}, u32[]{:S(2)}) %collective-permute-start) | collective-permute-done | bytes 1048608 | tf_op jit(solution)/shard_map/while/body/eval_jaxpr/ppermute | solution.py:19
  553.5 23.6 %collective-permute-done = f32[2,16,8192]{2,1,0:T(8,128)S(1)} collective-permute-done((f32[2,16,8192]{2,1,0:T(8,128)S(1)}, f32[2,16,8192]{2,1,0:T(8,128)S(1)}, u32[]{:S(2)}, u32[]{:S(2)}) %collective-permute-start) | collective-permute-done | bytes 1048608 | tf_op jit(solution)/shard_map/while/body/eval_jaxpr/ppermute | solution.py:19
  579.8 24.7 %collective-permute-done = f32[2,16,8192]{2,1,0:T(8,128)S(1)} collective-permute-done((f32[2,16,8192]{2,1,0:T(8,128)S(1)}, f32[2,16,8192]{2,1,0:T(8,128)S(1)}, u32[]{:S(2)}, u32[]{:S(2)}) %collective-permute-start) | collective-permute-done | bytes 1048608 | tf_op jit(solution)/shard_map/while/body/eval_jaxpr/ppermute | solution.py:19
  607.2 25.7 %collective-permute-done = f32[2,16,8192]{2,1,0:T(8,128)S(1)} collective-permute-done((f32[2,16,8192]{2,1,0:T(8,128)S(1)}, f32[2,16,8192]{2,1,0:T(8,128)S(1)}, u32[]{:S(2)}, u32[]{:S(2)}) %collective-permute-start) | collective-permute-done | bytes 1048608 | tf_op jit(solution)/shard_map/while/body/eval_jaxpr/ppermute | solution.py:19
  635.8 26.8 %collective-permute-done = f32[2,16,8192]{2,1,0:T(8,128)S(1)} collective-permute-done((f32[2,16,8192]{2,1,0:T(8,128)S(1)}, f32[2,16,8192]{2,1,0:T(8,128)S(1)}, u32[]{:S(2)}, u32[]{:S(2)}) %collective-permute-start) | collective-permute-done | bytes 1048608 | tf_op jit(solution)/shard_map/while/body/eval_jaxpr/ppermute | solution.py:19
  665.3 28.0 %collective-permute-done = f32[2,16,8192]{2,1,0:T(8,128)S(1)} collective-permute-done((f32[2,16,8192]{2,1,0:T(8,128)S(1)}, f32[2,16,8192]{2,1,0:T(8,128)S(1)}, u32[]{:S(2)}, u32[]{:S(2)}) %collective-permute-start) | collective-permute-done | bytes 1048608 | tf_op jit(solution)/shard_map/while/body/eval_jaxpr/ppermute | solution.py:19
  696.1 28.9 %collective-permute-done = f32[2,16,8192]{2,1,0:T(8,128)S(1)} collective-permute-done((f32[2,16,8192]{2,1,0:T(8,128)S(1)}, f32[2,16,8192]{2,1,0:T(8,128)S(1)}, u32[]{:S(2)}, u32[]{:S(2)}) %collective-permute-start) | collective-permute-done | bytes 1048608 | tf_op jit(solution)/shard_map/while/body/eval_jaxpr/ppermute | solution.py:19
  727.7 28.0 %collective-permute-done = f32[2,16,8192]{2,1,0:T(8,128)S(1)} collective-permute-done((f32[2,16,8192]{2,1,0:T(8,128)S(1)}, f32[2,16,8192]{2,1,0:T(8,128)S(1)}, u32[]{:S(2)}, u32[]{:S(2)}) %collective-permute-start) | collective-permute-done | bytes 1048608 | tf_op jit(solution)/shard_map/while/body/eval_jaxpr/ppermute | solution.py:19
  758.5 27.2 %collective-permute-done = f32[2,16,8192]{2,1,0:T(8,128)S(1)} collective-permute-done((f32[2,16,8192]{2,1,0:T(8,128)S(1)}, f32[2,16,8192]{2,1,0:T(8,128)S(1)}, u32[]{:S(2)}, u32[]{:S(2)}) %collective-permute-start) | collective-permute-done | bytes 1048608 | tf_op jit(solution)/shard_map/while/body/eval_jaxpr/ppermute | solution.py:19
  788.5 26.3 %collective-permute-done = f32[2,16,8192]{2,1,0:T(8,128)S(1)} collective-permute-done((f32[2,16,8192]{2,1,0:T(8,128)S(1)}, f32[2,16,8192]{2,1,0:T(8,128)S(1)}, u32[]{:S(2)}, u32[]{:S(2)}) %collective-permute-start) | collective-permute-done | bytes 1048608 | tf_op jit(solution)/shard_map/while/body/eval_jaxpr/ppermute | solution.py:19
  817.5 25.3 %collective-permute-done = f32[2,16,8192]{2,1,0:T(8,128)S(1)} collective-permute-done((f32[2,16,8192]{2,1,0:T(8,128)S(1)}, f32[2,16,8192]{2,1,0:T(8,128)S(1)}, u32[]{:S(2)}, u32[]{:S(2)}) %collective-permute-start) | collective-permute-done | bytes 1048608 | tf_op jit(solution)/shard_map/while/body/eval_jaxpr/ppermute | solution.py:19
  845.6 24.4 %collective-permute-done = f32[2,16,8192]{2,1,0:T(8,128)S(1)} collective-permute-done((f32[2,16,8192]{2,1,0:T(8,128)S(1)}, f32[2,16,8192]{2,1,0:T(8,128)S(1)}, u32[]{:S(2)}, u32[]{:S(2)}) %collective-permute-start) | collective-permute-done | bytes 1048608 | tf_op jit(solution)/shard_map/while/body/eval_jaxpr/ppermute | solution.py:19
  872.8 23.5 %collective-permute-done = f32[2,16,8192]{2,1,0:T(8,128)S(1)} collective-permute-done((f32[2,16,8192]{2,1,0:T(8,128)S(1)}, f32[2,16,8192]{2,1,0:T(8,128)S(1)}, u32[]{:S(2)}, u32[]{:S(2)}) %collective-permute-start) | collective-permute-done | bytes 1048608 | tf_op jit(solution)/shard_map/while/body/eval_jaxpr/ppermute | solution.py:19
  899.1 22.6 %collective-permute-done = f32[2,16,8192]{2,1,0:T(8,128)S(1)} collective-permute-done((f32[2,16,8192]{2,1,0:T(8,128)S(1)}, f32[2,16,8192]{2,1,0:T(8,128)S(1)}, u32[]{:S(2)}, u32[]{:S(2)}) %collective-permute-start) | collective-permute-done | bytes 1048608 | tf_op jit(solution)/shard_map/while/body/eval_jaxpr/ppermute | solution.py:19
  924.4 21.7 %collective-permute-done = f32[2,16,8192]{2,1,0:T(8,128)S(1)} collective-permute-done((f32[2,16,8192]{2,1,0:T(8,128)S(1)}, f32[2,16,8192]{2,1,0:T(8,128)S(1)}, u32[]{:S(2)}, u32[]{:S(2)}) %collective-permute-start) | collective-permute-done | bytes 1048608 | tf_op jit(solution)/shard_map/while/body/eval_jaxpr/ppermute | solution.py:19
  948.8 20.7 %collective-permute-done = f32[2,16,8192]{2,1,0:T(8,128)S(1)} collective-permute-done((f32[2,16,8192]{2,1,0:T(8,128)S(1)}, f32[2,16,8192]{2,1,0:T(8,128)S(1)}, u32[]{:S(2)}, u32[]{:S(2)}) %collective-permute-start) | collective-permute-done | bytes 1048608 | tf_op jit(solution)/shard_map/while/body/eval_jaxpr/ppermute | solution.py:19
  972.3 20.6 %collective-permute-done = f32[2,16,8192]{2,1,0:T(8,128)S(1)} collective-permute-done((f32[2,16,8192]{2,1,0:T(8,128)S(1)}, f32[2,16,8192]{2,1,0:T(8,128)S(1)}, u32[]{:S(2)}, u32[]{:S(2)}) %collective-permute-start) | collective-permute-done | bytes 1048608 | tf_op jit(solution)/shard_map/while/body/eval_jaxpr/ppermute | solution.py:19
  995.6 19.0 %collective-permute-done = f32[2,16,8192]{2,1,0:T(8,128)S(1)} collective-permute-done((f32[2,16,8192]{2,1,0:T(8,128)S(1)}, f32[2,16,8192]{2,1,0:T(8,128)S(1)}, u32[]{:S(2)}, u32[]{:S(2)}) %collective-permute-start) | collective-permute-done | bytes 1048608 | tf_op jit(solution)/shard_map/while/body/eval_jaxpr/ppermute | solution.py:19
  1017.4 17.8 %collective-permute-done = f32[2,16,8192]{2,1,0:T(8,128)S(1)} collective-permute-done((f32[2,16,8192]{2,1,0:T(8,128)S(1)}, f32[2,16,8192]{2,1,0:T(8,128)S(1)}, u32[]{:S(2)}, u32[]{:S(2)}) %collective-permute-start) | collective-permute-done | bytes 1048608 | tf_op jit(solution)/shard_map/while/body/eval_jaxpr/ppermute | solution.py:19
  1037.6 86.2 %while.55 = (s32[]{:T(128)}, f32[2,16,128,64]{2,3,1,0:T(8,128)}, f32[2,768,2048]{2,1,0:T(8,128)}, f32[2,768]{1,0:T(2,128)S(1)}, f32[2,32]{1,0:T(2,128)S(1)}, /*i...) while((s32[]{:T(128)}, f32[2,16,128,64]{2,3,1,0:T(8,128)}, ...), condition=%wide.region_11.12_spmd, body=%wide.region_9.11_spmd.sunk | while | flops 2443181312 | bytes 162972080 | solution.py:182
  1038.7 4.1 fusion.64
  1042.8 3.3 broadcast_multiply_fusion.2
  1053.0 7.2 fusion.65
  1060.2 6.8 copy.122
  1067.0 6.4 constant_dynamic-update-slice_fusion.2
  1073.5 4.4 fusion.66
  1081.8 4.1 fusion.64
  1085.9 3.3 broadcast_multiply_fusion.2
  1096.1 7.2 fusion.65
  1103.3 6.8 copy.122
  1110.1 6.4 constant_dynamic-update-slice_fusion.2
  1116.5 4.4 fusion.66
  1123.8 7.3 psum.7
  1131.1 8.4 fusion.30
  (290 shorter events, 190.2 us)
Async XLA Ops:
  0.7 19.8 %collective-permute-start.2 = (bf16[3,256]{1,0:T(4,128)(2,1)S(1)}, bf16[3,256]{1,0:T(4,128)(2,1)S(1)}, u32[]{:S(2)}, u32[]{:S(2)}) collective-permute-start(bf16[3,256]{1,0:T(4,128)(2,1)S(1)} %slice.159), channel_id=1, source_target_pairs={{0,4},{4,8},{8,12},{12,16},{16,20},{20,24},{24,28},{28,32},{32,36}... | collective-permute-start | bytes 4616 | tf_op jit(solution)/shard_map/ppermute | solution.py:19
  4.9 26.4 %collective-permute-start.1 = (bf16[3,2048]{1,0:T(4,128)(2,1)S(1)}, bf16[3,2048]{1,0:T(4,128)(2,1)S(1)}, u32[]{:S(2)}, u32[]{:S(2)}) collective-permute-start(bf16[3,2048]{1,0:T(4,128)(2,1)S(1)} %slice.149), channel_id=1, source_target_pairs={{0,4},{4,8},{8,12},{12,16},{16,20},{20,24},{24,28},{28,32},{32,36}... | collective-permute-start | bytes 36872 | tf_op jit(solution)/shard_map/ppermute | solution.py:19
  9.4 15.6 %collective-permute-start.3 = (bf16[3,256]{1,0:T(4,128)(2,1)S(1)}, bf16[3,256]{1,0:T(4,128)(2,1)S(1)}, u32[]{:S(2)}, u32[]{:S(2)}) collective-permute-start(bf16[3,256]{1,0:T(4,128)(2,1)S(1)} %slice.167), channel_id=1, source_target_pairs={{0,4},{4,8},{8,12},{12,16},{16,20},{20,24},{24,28},{28,32},{32,36}... | collective-permute-start | bytes 4616 | tf_op jit(solution)/shard_map/ppermute | solution.py:19
  31.3 18.1 %copy-start.22 = (f32[32]{0:T(128)S(1)}, f32[32]{0:T(128)}, u32[]{:S(2)}) copy-start(f32[32]{0:T(128)} %param.28) | copy-start | bytes 388
  66.1 7.8 copy-start.5
  79.9 14.4 %copy-start.7 = (bf16[1,768,256]{1,2,0:T(8,128)(2,1)S(1)}, bf16[1,768,256]{1,2,0:T(8,128)(2,1)}, u32[]{:S(2)}) copy-start(bf16[1,768,256]{1,2,0:T(8,128)(2,1)} %copy-done.6) | copy-start | bytes 1179652 | tf_op jit(solution)/shard_map/while
  80.0 14.8 %copy-start.2 = (bf16[1,768,2048]{1,2,0:T(8,128)(2,1)S(1)}, bf16[1,768,2048]{1,2,0:T(8,128)(2,1)}, u32[]{:S(2)}) copy-start(bf16[1,768,2048]{1,2,0:T(8,128)(2,1)} %copy.118) | copy-start | bytes 9437188 | tf_op jit(solution)/shard_map/while
  80.0 14.8 %copy-start.10 = (f32[16,768]{1,0:T(8,128)S(1)}, f32[16,768]{1,0:T(8,128)}, u32[]{:S(2)}) copy-start(f32[16,768]{1,0:T(8,128)} %get-tuple-element.578) | copy-start | bytes 147460 | tf_op jit(solution)/shard_map/while
  80.0 14.8 %copy-start.11 = (f32[16,768]{1,0:T(8,128)S(1)}, f32[16,768]{1,0:T(8,128)}, u32[]{:S(2)}) copy-start(f32[16,768]{1,0:T(8,128)} %get-tuple-element.579) | copy-start | bytes 147460 | tf_op jit(solution)/shard_map/while
  128.2 6.1 copy-start.4
  128.2 6.1 copy-start.12
  128.2 6.2 copy-start.9
  128.2 6.3 copy-start.19
  128.2 6.9 copy-start.23
  136.1 7.8 copy-start.5
  150.0 14.4 %copy-start.7 = (bf16[1,768,256]{1,2,0:T(8,128)(2,1)S(1)}, bf16[1,768,256]{1,2,0:T(8,128)(2,1)}, u32[]{:S(2)}) copy-start(bf16[1,768,256]{1,2,0:T(8,128)(2,1)} %copy-done.6) | copy-start | bytes 1179652 | tf_op jit(solution)/shard_map/while
  150.0 14.8 %copy-start.2 = (bf16[1,768,2048]{1,2,0:T(8,128)(2,1)S(1)}, bf16[1,768,2048]{1,2,0:T(8,128)(2,1)}, u32[]{:S(2)}) copy-start(bf16[1,768,2048]{1,2,0:T(8,128)(2,1)} %copy.118) | copy-start | bytes 9437188 | tf_op jit(solution)/shard_map/while
  150.1 14.8 %copy-start.10 = (f32[16,768]{1,0:T(8,128)S(1)}, f32[16,768]{1,0:T(8,128)}, u32[]{:S(2)}) copy-start(f32[16,768]{1,0:T(8,128)} %get-tuple-element.578) | copy-start | bytes 147460 | tf_op jit(solution)/shard_map/while
  150.1 14.8 %copy-start.11 = (f32[16,768]{1,0:T(8,128)S(1)}, f32[16,768]{1,0:T(8,128)}, u32[]{:S(2)}) copy-start(f32[16,768]{1,0:T(8,128)} %get-tuple-element.579) | copy-start | bytes 147460 | tf_op jit(solution)/shard_map/while
  198.3 6.1 copy-start.4
  198.3 6.1 copy-start.12
  198.3 6.2 copy-start.9
  198.3 6.3 copy-start.19
  198.3 6.9 copy-start.23
  219.6 29.0 %collective-permute-start = (f32[2,16,8192]{2,1,0:T(8,128)S(1)}, f32[2,16,8192]{2,1,0:T(8,128)S(1)}, u32[]{:S(2)}, u32[]{:S(2)}) collective-permute-start(f32[2,16,8192]{2,1,0:T(8,128)S(1)} %multiply_add_fusion.2), channel_id=1, source_target_pairs={{0,4},{4,8},{8,12},{12,16},{16,20},{20,24},{24,28},{28,32},{32,36}... | collective-permute-start | bytes 3145736 | tf_op jit(solution)/shard_map/while/body/eval_jaxpr/ppermute | solution.py:19
  249.4 28.0 %collective-permute-start = (f32[2,16,8192]{2,1,0:T(8,128)S(1)}, f32[2,16,8192]{2,1,0:T(8,128)S(1)}, u32[]{:S(2)}, u32[]{:S(2)}) collective-permute-start(f32[2,16,8192]{2,1,0:T(8,128)S(1)} %multiply_add_fusion.2), channel_id=1, source_target_pairs={{0,4},{4,8},{8,12},{12,16},{16,20},{20,24},{24,28},{28,32},{32,36}... | collective-permute-start | bytes 3145736 | tf_op jit(solution)/shard_map/while/body/eval_jaxpr/ppermute | solution.py:19
  278.3 27.1 %collective-permute-start = (f32[2,16,8192]{2,1,0:T(8,128)S(1)}, f32[2,16,8192]{2,1,0:T(8,128)S(1)}, u32[]{:S(2)}, u32[]{:S(2)}) collective-permute-start(f32[2,16,8192]{2,1,0:T(8,128)S(1)} %multiply_add_fusion.2), channel_id=1, source_target_pairs={{0,4},{4,8},{8,12},{12,16},{16,20},{20,24},{24,28},{28,32},{32,36}... | collective-permute-start | bytes 3145736 | tf_op jit(solution)/shard_map/while/body/eval_jaxpr/ppermute | solution.py:19
  306.2 26.2 %collective-permute-start = (f32[2,16,8192]{2,1,0:T(8,128)S(1)}, f32[2,16,8192]{2,1,0:T(8,128)S(1)}, u32[]{:S(2)}, u32[]{:S(2)}) collective-permute-start(f32[2,16,8192]{2,1,0:T(8,128)S(1)} %multiply_add_fusion.2), channel_id=1, source_target_pairs={{0,4},{4,8},{8,12},{12,16},{16,20},{20,24},{24,28},{28,32},{32,36}... | collective-permute-start | bytes 3145736 | tf_op jit(solution)/shard_map/while/body/eval_jaxpr/ppermute | solution.py:19
  333.2 25.3 %collective-permute-start = (f32[2,16,8192]{2,1,0:T(8,128)S(1)}, f32[2,16,8192]{2,1,0:T(8,128)S(1)}, u32[]{:S(2)}, u32[]{:S(2)}) collective-permute-start(f32[2,16,8192]{2,1,0:T(8,128)S(1)} %multiply_add_fusion.2), channel_id=1, source_target_pairs={{0,4},{4,8},{8,12},{12,16},{16,20},{20,24},{24,28},{28,32},{32,36}... | collective-permute-start | bytes 3145736 | tf_op jit(solution)/shard_map/while/body/eval_jaxpr/ppermute | solution.py:19
  359.3 24.3 %collective-permute-start = (f32[2,16,8192]{2,1,0:T(8,128)S(1)}, f32[2,16,8192]{2,1,0:T(8,128)S(1)}, u32[]{:S(2)}, u32[]{:S(2)}) collective-permute-start(f32[2,16,8192]{2,1,0:T(8,128)S(1)} %multiply_add_fusion.2), channel_id=1, source_target_pairs={{0,4},{4,8},{8,12},{12,16},{16,20},{20,24},{24,28},{28,32},{32,36}... | collective-permute-start | bytes 3145736 | tf_op jit(solution)/shard_map/while/body/eval_jaxpr/ppermute | solution.py:19
  384.5 23.4 %collective-permute-start = (f32[2,16,8192]{2,1,0:T(8,128)S(1)}, f32[2,16,8192]{2,1,0:T(8,128)S(1)}, u32[]{:S(2)}, u32[]{:S(2)}) collective-permute-start(f32[2,16,8192]{2,1,0:T(8,128)S(1)} %multiply_add_fusion.2), channel_id=1, source_target_pairs={{0,4},{4,8},{8,12},{12,16},{16,20},{20,24},{24,28},{28,32},{32,36}... | collective-permute-start | bytes 3145736 | tf_op jit(solution)/shard_map/while/body/eval_jaxpr/ppermute | solution.py:19
  408.8 22.5 %collective-permute-start = (f32[2,16,8192]{2,1,0:T(8,128)S(1)}, f32[2,16,8192]{2,1,0:T(8,128)S(1)}, u32[]{:S(2)}, u32[]{:S(2)}) collective-permute-start(f32[2,16,8192]{2,1,0:T(8,128)S(1)} %multiply_add_fusion.2), channel_id=1, source_target_pairs={{0,4},{4,8},{8,12},{12,16},{16,20},{20,24},{24,28},{28,32},{32,36}... | collective-permute-start | bytes 3145736 | tf_op jit(solution)/shard_map/while/body/eval_jaxpr/ppermute | solution.py:19
  432.1 22.5 %collective-permute-start = (f32[2,16,8192]{2,1,0:T(8,128)S(1)}, f32[2,16,8192]{2,1,0:T(8,128)S(1)}, u32[]{:S(2)}, u32[]{:S(2)}) collective-permute-start(f32[2,16,8192]{2,1,0:T(8,128)S(1)} %multiply_add_fusion.2), channel_id=1, source_target_pairs={{0,4},{4,8},{8,12},{12,16},{16,20},{20,24},{24,28},{28,32},{32,36}... | collective-permute-start | bytes 3145736 | tf_op jit(solution)/shard_map/while/body/eval_jaxpr/ppermute | solution.py:19
  455.4 22.5 %collective-permute-start = (f32[2,16,8192]{2,1,0:T(8,128)S(1)}, f32[2,16,8192]{2,1,0:T(8,128)S(1)}, u32[]{:S(2)}, u32[]{:S(2)}) collective-permute-start(f32[2,16,8192]{2,1,0:T(8,128)S(1)} %multiply_add_fusion.2), channel_id=1, source_target_pairs={{0,4},{4,8},{8,12},{12,16},{16,20},{20,24},{24,28},{28,32},{32,36}... | collective-permute-start | bytes 3145736 | tf_op jit(solution)/shard_map/while/body/eval_jaxpr/ppermute | solution.py:19
  478.8 22.5 %collective-permute-start = (f32[2,16,8192]{2,1,0:T(8,128)S(1)}, f32[2,16,8192]{2,1,0:T(8,128)S(1)}, u32[]{:S(2)}, u32[]{:S(2)}) collective-permute-start(f32[2,16,8192]{2,1,0:T(8,128)S(1)} %multiply_add_fusion.2), channel_id=1, source_target_pairs={{0,4},{4,8},{8,12},{12,16},{16,20},{20,24},{24,28},{28,32},{32,36}... | collective-permute-start | bytes 3145736 | tf_op jit(solution)/shard_map/while/body/eval_jaxpr/ppermute | solution.py:19
  502.1 23.3 %collective-permute-start = (f32[2,16,8192]{2,1,0:T(8,128)S(1)}, f32[2,16,8192]{2,1,0:T(8,128)S(1)}, u32[]{:S(2)}, u32[]{:S(2)}) collective-permute-start(f32[2,16,8192]{2,1,0:T(8,128)S(1)} %multiply_add_fusion.2), channel_id=1, source_target_pairs={{0,4},{4,8},{8,12},{12,16},{16,20},{20,24},{24,28},{28,32},{32,36}... | collective-permute-start | bytes 3145736 | tf_op jit(solution)/shard_map/while/body/eval_jaxpr/ppermute | solution.py:19
  526.3 24.4 %collective-permute-start = (f32[2,16,8192]{2,1,0:T(8,128)S(1)}, f32[2,16,8192]{2,1,0:T(8,128)S(1)}, u32[]{:S(2)}, u32[]{:S(2)}) collective-permute-start(f32[2,16,8192]{2,1,0:T(8,128)S(1)} %multiply_add_fusion.2), channel_id=1, source_target_pairs={{0,4},{4,8},{8,12},{12,16},{16,20},{20,24},{24,28},{28,32},{32,36}... | collective-permute-start | bytes 3145736 | tf_op jit(solution)/shard_map/while/body/eval_jaxpr/ppermute | solution.py:19
  551.5 25.5 %collective-permute-start = (f32[2,16,8192]{2,1,0:T(8,128)S(1)}, f32[2,16,8192]{2,1,0:T(8,128)S(1)}, u32[]{:S(2)}, u32[]{:S(2)}) collective-permute-start(f32[2,16,8192]{2,1,0:T(8,128)S(1)} %multiply_add_fusion.2), channel_id=1, source_target_pairs={{0,4},{4,8},{8,12},{12,16},{16,20},{20,24},{24,28},{28,32},{32,36}... | collective-permute-start | bytes 3145736 | tf_op jit(solution)/shard_map/while/body/eval_jaxpr/ppermute | solution.py:19
  577.9 26.6 %collective-permute-start = (f32[2,16,8192]{2,1,0:T(8,128)S(1)}, f32[2,16,8192]{2,1,0:T(8,128)S(1)}, u32[]{:S(2)}, u32[]{:S(2)}) collective-permute-start(f32[2,16,8192]{2,1,0:T(8,128)S(1)} %multiply_add_fusion.2), channel_id=1, source_target_pairs={{0,4},{4,8},{8,12},{12,16},{16,20},{20,24},{24,28},{28,32},{32,36}... | collective-permute-start | bytes 3145736 | tf_op jit(solution)/shard_map/while/body/eval_jaxpr/ppermute | solution.py:19
  605.3 27.7 %collective-permute-start = (f32[2,16,8192]{2,1,0:T(8,128)S(1)}, f32[2,16,8192]{2,1,0:T(8,128)S(1)}, u32[]{:S(2)}, u32[]{:S(2)}) collective-permute-start(f32[2,16,8192]{2,1,0:T(8,128)S(1)} %multiply_add_fusion.2), channel_id=1, source_target_pairs={{0,4},{4,8},{8,12},{12,16},{16,20},{20,24},{24,28},{28,32},{32,36}... | collective-permute-start | bytes 3145736 | tf_op jit(solution)/shard_map/while/body/eval_jaxpr/ppermute | solution.py:19
  633.8 28.8 %collective-permute-start = (f32[2,16,8192]{2,1,0:T(8,128)S(1)}, f32[2,16,8192]{2,1,0:T(8,128)S(1)}, u32[]{:S(2)}, u32[]{:S(2)}) collective-permute-start(f32[2,16,8192]{2,1,0:T(8,128)S(1)} %multiply_add_fusion.2), channel_id=1, source_target_pairs={{0,4},{4,8},{8,12},{12,16},{16,20},{20,24},{24,28},{28,32},{32,36}... | collective-permute-start | bytes 3145736 | tf_op jit(solution)/shard_map/while/body/eval_jaxpr/ppermute | solution.py:19
  663.4 29.9 %collective-permute-start = (f32[2,16,8192]{2,1,0:T(8,128)S(1)}, f32[2,16,8192]{2,1,0:T(8,128)S(1)}, u32[]{:S(2)}, u32[]{:S(2)}) collective-permute-start(f32[2,16,8192]{2,1,0:T(8,128)S(1)} %multiply_add_fusion.2), channel_id=1, source_target_pairs={{0,4},{4,8},{8,12},{12,16},{16,20},{20,24},{24,28},{28,32},{32,36}... | collective-permute-start | bytes 3145736 | tf_op jit(solution)/shard_map/while/body/eval_jaxpr/ppermute | solution.py:19
  694.1 30.8 %collective-permute-start = (f32[2,16,8192]{2,1,0:T(8,128)S(1)}, f32[2,16,8192]{2,1,0:T(8,128)S(1)}, u32[]{:S(2)}, u32[]{:S(2)}) collective-permute-start(f32[2,16,8192]{2,1,0:T(8,128)S(1)} %multiply_add_fusion.2), channel_id=1, source_target_pairs={{0,4},{4,8},{8,12},{12,16},{16,20},{20,24},{24,28},{28,32},{32,36}... | collective-permute-start | bytes 3145736 | tf_op jit(solution)/shard_map/while/body/eval_jaxpr/ppermute | solution.py:19
  725.8 30.0 %collective-permute-start = (f32[2,16,8192]{2,1,0:T(8,128)S(1)}, f32[2,16,8192]{2,1,0:T(8,128)S(1)}, u32[]{:S(2)}, u32[]{:S(2)}) collective-permute-start(f32[2,16,8192]{2,1,0:T(8,128)S(1)} %multiply_add_fusion.2), channel_id=1, source_target_pairs={{0,4},{4,8},{8,12},{12,16},{16,20},{20,24},{24,28},{28,32},{32,36}... | collective-permute-start | bytes 3145736 | tf_op jit(solution)/shard_map/while/body/eval_jaxpr/ppermute | solution.py:19
  756.6 29.1 %collective-permute-start = (f32[2,16,8192]{2,1,0:T(8,128)S(1)}, f32[2,16,8192]{2,1,0:T(8,128)S(1)}, u32[]{:S(2)}, u32[]{:S(2)}) collective-permute-start(f32[2,16,8192]{2,1,0:T(8,128)S(1)} %multiply_add_fusion.2), channel_id=1, source_target_pairs={{0,4},{4,8},{8,12},{12,16},{16,20},{20,24},{24,28},{28,32},{32,36}... | collective-permute-start | bytes 3145736 | tf_op jit(solution)/shard_map/while/body/eval_jaxpr/ppermute | solution.py:19
  786.5 28.2 %collective-permute-start = (f32[2,16,8192]{2,1,0:T(8,128)S(1)}, f32[2,16,8192]{2,1,0:T(8,128)S(1)}, u32[]{:S(2)}, u32[]{:S(2)}) collective-permute-start(f32[2,16,8192]{2,1,0:T(8,128)S(1)} %multiply_add_fusion.2), channel_id=1, source_target_pairs={{0,4},{4,8},{8,12},{12,16},{16,20},{20,24},{24,28},{28,32},{32,36}... | collective-permute-start | bytes 3145736 | tf_op jit(solution)/shard_map/while/body/eval_jaxpr/ppermute | solution.py:19
  815.6 27.3 %collective-permute-start = (f32[2,16,8192]{2,1,0:T(8,128)S(1)}, f32[2,16,8192]{2,1,0:T(8,128)S(1)}, u32[]{:S(2)}, u32[]{:S(2)}) collective-permute-start(f32[2,16,8192]{2,1,0:T(8,128)S(1)} %multiply_add_fusion.2), channel_id=1, source_target_pairs={{0,4},{4,8},{8,12},{12,16},{16,20},{20,24},{24,28},{28,32},{32,36}... | collective-permute-start | bytes 3145736 | tf_op jit(solution)/shard_map/while/body/eval_jaxpr/ppermute | solution.py:19
  843.7 26.4 %collective-permute-start = (f32[2,16,8192]{2,1,0:T(8,128)S(1)}, f32[2,16,8192]{2,1,0:T(8,128)S(1)}, u32[]{:S(2)}, u32[]{:S(2)}) collective-permute-start(f32[2,16,8192]{2,1,0:T(8,128)S(1)} %multiply_add_fusion.2), channel_id=1, source_target_pairs={{0,4},{4,8},{8,12},{12,16},{16,20},{20,24},{24,28},{28,32},{32,36}... | collective-permute-start | bytes 3145736 | tf_op jit(solution)/shard_map/while/body/eval_jaxpr/ppermute | solution.py:19
  870.9 25.4 %collective-permute-start = (f32[2,16,8192]{2,1,0:T(8,128)S(1)}, f32[2,16,8192]{2,1,0:T(8,128)S(1)}, u32[]{:S(2)}, u32[]{:S(2)}) collective-permute-start(f32[2,16,8192]{2,1,0:T(8,128)S(1)} %multiply_add_fusion.2), channel_id=1, source_target_pairs={{0,4},{4,8},{8,12},{12,16},{16,20},{20,24},{24,28},{28,32},{32,36}... | collective-permute-start | bytes 3145736 | tf_op jit(solution)/shard_map/while/body/eval_jaxpr/ppermute | solution.py:19
  897.1 24.5 %collective-permute-start = (f32[2,16,8192]{2,1,0:T(8,128)S(1)}, f32[2,16,8192]{2,1,0:T(8,128)S(1)}, u32[]{:S(2)}, u32[]{:S(2)}) collective-permute-start(f32[2,16,8192]{2,1,0:T(8,128)S(1)} %multiply_add_fusion.2), channel_id=1, source_target_pairs={{0,4},{4,8},{8,12},{12,16},{16,20},{20,24},{24,28},{28,32},{32,36}... | collective-permute-start | bytes 3145736 | tf_op jit(solution)/shard_map/while/body/eval_jaxpr/ppermute | solution.py:19
  922.5 23.6 %collective-permute-start = (f32[2,16,8192]{2,1,0:T(8,128)S(1)}, f32[2,16,8192]{2,1,0:T(8,128)S(1)}, u32[]{:S(2)}, u32[]{:S(2)}) collective-permute-start(f32[2,16,8192]{2,1,0:T(8,128)S(1)} %multiply_add_fusion.2), channel_id=1, source_target_pairs={{0,4},{4,8},{8,12},{12,16},{16,20},{20,24},{24,28},{28,32},{32,36}... | collective-permute-start | bytes 3145736 | tf_op jit(solution)/shard_map/while/body/eval_jaxpr/ppermute | solution.py:19
  946.9 22.7 %collective-permute-start = (f32[2,16,8192]{2,1,0:T(8,128)S(1)}, f32[2,16,8192]{2,1,0:T(8,128)S(1)}, u32[]{:S(2)}, u32[]{:S(2)}) collective-permute-start(f32[2,16,8192]{2,1,0:T(8,128)S(1)} %multiply_add_fusion.2), channel_id=1, source_target_pairs={{0,4},{4,8},{8,12},{12,16},{16,20},{20,24},{24,28},{28,32},{32,36}... | collective-permute-start | bytes 3145736 | tf_op jit(solution)/shard_map/while/body/eval_jaxpr/ppermute | solution.py:19
  970.4 22.5 %collective-permute-start = (f32[2,16,8192]{2,1,0:T(8,128)S(1)}, f32[2,16,8192]{2,1,0:T(8,128)S(1)}, u32[]{:S(2)}, u32[]{:S(2)}) collective-permute-start(f32[2,16,8192]{2,1,0:T(8,128)S(1)} %multiply_add_fusion.2), channel_id=1, source_target_pairs={{0,4},{4,8},{8,12},{12,16},{16,20},{20,24},{24,28},{28,32},{32,36}... | collective-permute-start | bytes 3145736 | tf_op jit(solution)/shard_map/while/body/eval_jaxpr/ppermute | solution.py:19
  993.7 20.9 %collective-permute-start = (f32[2,16,8192]{2,1,0:T(8,128)S(1)}, f32[2,16,8192]{2,1,0:T(8,128)S(1)}, u32[]{:S(2)}, u32[]{:S(2)}) collective-permute-start(f32[2,16,8192]{2,1,0:T(8,128)S(1)} %multiply_add_fusion.2), channel_id=1, source_target_pairs={{0,4},{4,8},{8,12},{12,16},{16,20},{20,24},{24,28},{28,32},{32,36}... | collective-permute-start | bytes 3145736 | tf_op jit(solution)/shard_map/while/body/eval_jaxpr/ppermute | solution.py:19
  1015.4 19.7 %collective-permute-start = (f32[2,16,8192]{2,1,0:T(8,128)S(1)}, f32[2,16,8192]{2,1,0:T(8,128)S(1)}, u32[]{:S(2)}, u32[]{:S(2)}) collective-permute-start(f32[2,16,8192]{2,1,0:T(8,128)S(1)} %multiply_add_fusion.2), channel_id=1, source_target_pairs={{0,4},{4,8},{8,12},{12,16},{16,20},{20,24},{24,28},{28,32},{32,36}... | collective-permute-start | bytes 3145736 | tf_op jit(solution)/shard_map/while/body/eval_jaxpr/ppermute | solution.py:19
  1037.6 93.5 %copy-start.17 = (f32[2048]{0:T(1024)S(1)}, f32[2048]{0:T(1024)}, u32[]{:S(2)}) copy-start(f32[2048]{0:T(1024)} %convert_element_type.125) | copy-start | bytes 24580
  1038.7 7.4 slice-start.2
  1060.2 13.2 %slice-start = ((s8[6291456]{0:T(1024)(128)(4,1)}), s8[2097152]{0:T(1024)(128)(4,1)S(1)}, s32[]{:S(2)}) async-start(s8[6291456]{0:T(1024)(128)(4,1)} %bitcast.247), calls=%async_computation | async-start | bytes 4194304 | tf_op jit(solution)/shard_map/while
  1067.0 6.4 slice-start.1
  1067.0 6.4 copy-start.1
  1081.8 7.4 slice-start.2
  1103.3 13.2 %slice-start = ((s8[6291456]{0:T(1024)(128)(4,1)}), s8[2097152]{0:T(1024)(128)(4,1)S(1)}, s32[]{:S(2)}) async-start(s8[6291456]{0:T(1024)(128)(4,1)} %bitcast.247), calls=%async_computation | async-start | bytes 4194304 | tf_op jit(solution)/shard_map/while
  1110.1 6.4 slice-start.1
  1110.1 6.4 copy-start.1
  (21 other events, 47.2 us)
where the time goes:
time: 1150 us; the launch traced here: 1140 us
  waiting for transfers between devices  729 us (63%)
  other arithmetic  140 us (12%)
  local copies, waits for them, and re-layouts  91.8 us (8%)
  matrix products  80.1 us (7%)
  starting transfers between devices  72 us (6%)
  loops' own time  19.4 us (2%)
    ppermute x34, waiting for transfers between devices, passed_along(): return lax.ppermute(x, axis, pairs)  729 us
    ppermute x34, starting transfers between devices, passed_along(): return lax.ppermute(x, axis, pairs)  72 us
    dot_general x4, matrix products, block_terms(): jnp.einsum('kij,jkp->ikp', weights, x_heads[:, group_index], preferred_el...  54.8 us
    dynamic_slice x26, local copies, waits for them, and re-layouts, shards(): lax.map(first_pass, (x_conv.reshape(block_count, Q, -1), b_conv.reshape(b...  33.1 us
    convert_element_type x3, other arithmetic, conv_silu(): return jax.nn.silu(summed).astype(jnp.bfloat16)  27.7 us
    dynamic_update_slice x8, local copies, waits for them, and re-layouts, shards(): lax.map(first_pass, (x_conv.reshape(block_count, Q, -1), b_conv.reshape(b...  26.6 us
    add x31, other arithmetic, relay(): dev_factor[:, :, None] * incoming + flat_state  25.7 us
  transfers between devices with their start and end apart: 34, of which 31 were waited for; matrix products, arithmetic and copies ran while one was open for 2% of the time, Pallas kernels for 0%

commit v1 on v0

v1 whole, which is shorter than its diff:
```python
import functools
import math

import jax
import jax.numpy as jnp
from jax import lax
from jax.experimental import pallas as pl
from jax.experimental.pallas import tpu as pltpu
from jax.sharding import PartitionSpec as P

F32 = jnp.float32
BF16 = jnp.bfloat16
P_SIZE = 64
N = 128
K = 4
L = 128
TILE = 256
EPS = 1e-05
LOG2E = math.log2(math.e)
HI = lax.Precision.HIGHEST
MESH = pl.DeviceIdType.MESH
PIECES = 32
ROWS = 80
FIRST_PART = 13


def silu(v):
    return v * (0.5 + 0.5 * jnp.tanh(0.5 * v))


def split3(v):
    hi = v.astype(BF16)
    rest = v - hi.astype(F32)
    mid = rest.astype(BF16)
    low = (rest - mid.astype(F32)).astype(BF16)
    return hi, mid, low


def wide3(v):
    return jnp.concatenate([p.astype(F32) for p in split3(v)], axis=1).astype(BF16)


def dot(a, b, **kw):
    return jnp.dot(a, b, preferred_element_type=F32, **kw)


def kernel(
    n_ctx,
    n_head,
    chunks,
    x_hbm,
    b_hbm,
    c_hbm,
    gate_hbm,
    taps_x,
    taps_b,
    taps_c,
    step_ref,
    rate_ref,
    skip_ref,
    doc_ref,
    gated_hbm,
    scale_ref,
    xbuf,
    bcbuf,
    gate_buf,
    xconv,
    bconv,
    cconv,
    yint,
    prefix,
    state,
    pcar,
    cum_s,
    cumt_s,
    allow_s,
    emask_s,
    sel,
    band,
    tril,
    send1,
    recv1,
    send2,
    recv2,
    sums,
    sums_recv,
    x_sem,
    bc_sem,
    gate_sem,
    out_sem,
    halo_ssem,
    halo_rsem,
    ssem1,
    rsem1,
    ssem2,
    rsem2,
    sum_ssem,
    sum_rsem,
):
    me = lax.axis_index("ctx")
    my_head = lax.axis_index("head")
    rows = chunks * L
    heads = step_ref.shape[1]
    per_dev = PIECES // n_ctx

    def x_copy(c):
        r = pl.ds(pl.multiple_of(c * L, L), L)
        d = pl.ds(pl.multiple_of(c * L + L, L), L)
        return pltpu.make_async_copy(x_hbm.at[r, :], xbuf.at[d, :], x_sem.at[c])

    def gate_copy(c):
        r = pl.ds(pl.multiple_of(c * L, L), L)
        return pltpu.make_async_copy(gate_hbm.at[r, :], gate_buf.at[r, :], gate_sem.at[c])

    b_copy = pltpu.make_async_copy(b_hbm, bcbuf.at[0, pl.ds(L, rows), :], bc_sem.at[0])
    c_copy = pltpu.make_async_copy(c_hbm, bcbuf.at[1, pl.ds(L, rows), :], bc_sem.at[1])
    b_copy.start()
    c_copy.start()

    def start_x(c, _):
        x_copy(c).start()
        return 0

    lax.fori_loop(0, chunks, start_x, 0)

    barrier = pltpu.get_barrier_semaphore()

    def greet_ctx(s, _):
        pl.semaphore_signal(
            barrier, inc=1, device_id={"ctx": lax.rem(me + s, n_ctx)}, device_id_type=MESH
        )
        return 0

    def greet_head(s, _):
        pl.semaphore_signal(
            barrier, inc=1, device_id={"head": lax.rem(my_head + s, n_head)}, device_id_type=MESH
        )
        return 0

    lax.fori_loop(1, n_ctx, greet_ctx, 0)
    lax.fori_loop(1, n_head, greet_head, 0)

    sel_row = lax.broadcasted_iota(jnp.int32, sel.shape, 0)
    sel_lane = lax.broadcasted_iota(jnp.int32, sel.shape, 1)
    sel[...] = jnp.where(
        lax.rem(sel_row, heads) == lax.div(sel_lane, P_SIZE), 1.0, 0.0
    ).astype(BF16)
    t_iota = lax.broadcasted_iota(jnp.int32, (L, L), 0)
    q_iota = lax.broadcasted_iota(jnp.int32, (L, L), 1)
    for s in range(1, K):
        band[s - 1, 0] = jnp.where(q_iota == t_iota + L - s, 1.0, 0.0)
        band[s - 1, 1] = jnp.where(q_iota == t_iota - s, 1.0, 0.0)
    tril[...] = jnp.where(t_iota >= q_iota, 1.0, 0.0)
    xbuf[0 : L - 16, :] = jnp.zeros((L - 16, xbuf.shape[1]), BF16)
    bcbuf[:, 0 : L - 16, :] = jnp.zeros((2, L - 16, bcbuf.shape[2]), BF16)
    state[...] = jnp.zeros_like(state)
    sums[...] = jnp.zeros_like(sums)

    pl.semaphore_wait(barrier, n_ctx + n_head - 2)

    rim = pl.ds(rows - 16, 16)
    spot = pl.ds(L - 16, 16)

    def halo(i):
        src = (x_hbm, b_hbm, c_hbm)[i].at[rim, :]
        dst = xbuf.at[spot, :] if i == 0 else bcbuf.at[i - 1, spot, :]
        return pltpu.make_async_remote_copy(
            src_ref=src,
            dst_ref=dst,
            send_sem=halo_ssem.at[i],
            recv_sem=halo_rsem.at[i],
            device_id={"ctx": lax.rem(me + 1, n_ctx)},
            device_id_type=MESH,
        )

    for i in range(3):
        halo(i).start()

    def start_gate(c, _):
        gate_copy(c).start()
        return 0

    lax.fori_loop(0, chunks, start_gate, 0)

    docs = [doc_ref[d] for d in range(doc_ref.shape[0])]

    def seg(pos):
        total = jnp.where(pos >= docs[0], 1, 0)
        for d in docs[1:]:
            total = total + jnp.where(pos >= d, 1, 0)
        return total

    b_copy.wait()
    c_copy.wait()
    for i in range(3):
        halo(i).wait_recv()

    def first(c, _):
        x_copy(c).wait()
        base = me * rows + c * L
        seg_t = seg(base + t_iota)
        seg_cur = seg(base + q_iota)
        seg_old = seg(base - L + q_iota)
        same_cur = seg_t == seg_cur
        same_old = seg_t == seg_old
        shifts = jnp.concatenate(
            [
                jnp.concatenate(
                    [
                        jnp.where(same_old, band[s, 0], 0.0),
                        jnp.where(same_cur, band[s, 1], 0.0),
                    ],
                    axis=1,
                ).astype(BF16)
                for s in range(K - 1)
            ],
            axis=0,
        )
        allow_s[c] = jnp.where(same_cur, tril[...], 0.0)
        window = pl.ds(pl.multiple_of(c * L, L), 2 * L)

        def conv(win, taps):
            moved = dot(shifts, win)
            v = moved[2 * L : 3 * L] * taps[0:1]
            v = v + moved[L : 2 * L] * taps[1:2]
            v = v + moved[0:L] * taps[2:3]
            v = v + win[L : 2 * L].astype(F32) * taps[3:4]
            return silu(v)

        b_now = conv(bcbuf[0, window, :], taps_b[...].astype(F32))
        c_now = conv(bcbuf[1, window, :], taps_c[...].astype(F32))
        groups = b_now.shape[1] // N
        b_t = []
        for g in range(groups):
            lanes = slice(g * N, (g + 1) * N)
            bconv[c * groups + g] = b_now[:, lanes].astype(BF16)
            cconv[c * groups + g] = c_now[:, lanes].astype(BF16)
            b_t.append(b_now[:, lanes].T.astype(BF16))

        step = step_ref[pl.ds(pl.multiple_of(c * L, L), L), :]
        cum = dot(tril[...], step * (rate_ref[...] * -LOG2E), precision=HI)
        cum_j = cum - jnp.log(step) * LOG2E
        cum_jt = cum_j.T
        per_group = heads // groups
        for g in range(groups):
            hs = slice(g * per_group, (g + 1) * per_group)
            cum_s[c * groups + g] = cum[:, hs]
            cumt_s[c * groups + g] = cum_jt[hs, :]
        seg_last = seg(base + L - 1)
        seg_before = seg(base - 1)
        cum_last = cum[L - 1 : L, :]
        h_iota = lax.broadcasted_iota(jnp.int32, (L, heads), 0)
        seg_h = seg(base + h_iota)
        weight = jnp.where(seg_h == seg_last, jnp.exp2(cum_last - cum_j), 0.0)
        emask_s[c] = jnp.where(seg_h == seg_before, jnp.exp2(cum), 0.0)
        carry = jnp.where(seg_last == seg_before, jnp.exp2(cum_last), 0.0)
        left = wide3(
            jnp.concatenate([weight, jnp.broadcast_to(carry, (16, heads))], axis=0)
        )
        for tile in range(x_hbm.shape[1] // TILE):
            lanes = slice(tile * TILE, (tile + 1) * TILE)
            g, at = divmod(tile * TILE, per_group * P_SIZE)
            here = slice(at, at + TILE)
            x_now = conv(xbuf[window, lanes], taps_x[:, lanes].astype(F32)).astype(BF16)
            xconv[c * groups + g, :, here] = x_now
            spread = dot(left, sel[:, lanes])
            x_weighted = (x_now.astype(F32) * spread[0:L]).astype(BF16)
            local = dot(b_t[g], x_weighted)
            factor = spread[L : L + 8]
            before = state[g, :, here]
            prefix[c * groups + g, :, here] = before
            state[g, :, here] = before * factor[0:1] + local
            old = jnp.where(c == 0, 1.0, pcar[c, :, lanes])
            pcar[c, :, lanes] = old
            pcar[c + 1, :, lanes] = old * factor
        return 0

    lax.fori_loop(0, chunks, first, 0)
    groups = bconv.shape[0] // chunks
    per_group = heads // groups

    r_iota = lax.broadcasted_iota(jnp.int32, (16, 128), 0)
    for pair in range(PIECES // 2):
        g, at = divmod(pair * 128, per_group * P_SIZE)
        hi, mid, low = split3(
            jnp.broadcast_to(pcar[chunks, 0:1, pair * 128 : (pair + 1) * 128], (16, 128))
        )
        tail = jnp.where(
            r_iota == 0,
            hi.astype(F32),
            jnp.where(r_iota == 1, mid.astype(F32), jnp.where(r_iota == 2, low.astype(F32), 0.0)),
        ).astype(BF16)
        for half in range(2):
            k = pair * 2 + half
            send1[k // per_dev, k % per_dev, 0:64, :] = state[
                g, half * 64 : (half + 1) * 64, at : at + 128
            ].astype(BF16)
            send1[k // per_dev, k % per_dev, 64:80, :] = tail

    def copy1(other, slot):
        return pltpu.make_async_remote_copy(
            src_ref=send1.at[other],
            dst_ref=recv1.at[slot],
            send_sem=ssem1.at[other],
            recv_sem=rsem1.at[slot],
            device_id={"ctx": other},
            device_id_type=MESH,
        )

    def copy2(other, slot):
        return pltpu.make_async_remote_copy(
            src_ref=send2.at[other],
            dst_ref=recv2.at[slot],
            send_sem=ssem2.at[other],
            recv_sem=rsem2.at[slot],
            device_id={"ctx": other},
            device_id_type=MESH,
        )

    def send_state(s, _):
        copy1(lax.rem(me + s, n_ctx), me).start()
        return 0

    lax.fori_loop(1, n_ctx, send_state, 0)
    recv1[me] = send1[me]

    lane = lax.broadcasted_iota(jnp.int32, (L, 128), 1)

    def second(i, _):
        c = lax.div(i, groups)
        scores = lax.dot_general(
            cconv[i], bconv[i], (((1,), (1,)), ((), ())), preferred_element_type=F32
        )
        scores = scores * allow_s[c]
        cum = cum_s[i]
        for pair in range(per_group // 2):
            ws = []
            for h in (2 * pair, 2 * pair + 1):
                gap = cum[:, h : h + 1] - cumt_s[i, h : h + 1, :]
                ws.append((scores * jnp.exp2(jnp.minimum(gap, 4.0))).astype(BF16))
            x_pair = xconv[i, :, pair * 128 : (pair + 1) * 128]
            zero = jnp.zeros_like(x_pair)
            both = jnp.concatenate(
                [jnp.where(lane < P_SIZE, x_pair, zero), jnp.where(lane < P_SIZE, zero, x_pair)],
                axis=0,
            )
            yint[i, :, pair * 128 : (pair + 1) * 128] = dot(jnp.concatenate(ws, axis=1), both)
        return 0

    lax.fori_loop(0, FIRST_PART, second, 0)

    def scan(e, acc):
        @pl.when(e != me)
        def _():
            copy1(e, e).wait_recv()

        out = []
        for k in range(per_dev):
            send2[e, k] = acc[k].astype(BF16)
            got = recv1[e, k].astype(F32)
            factor = got[64:65] + got[65:66] + got[66:67]
            out.append(acc[k] * factor + got[0:64])

        @pl.when(e != me)
        def _():
            copy2(e, me).start()

        @pl.when(e == me)
        def _():
            recv2[me] = send2[me]

        return tuple(out)

    lax.fori_loop(
        0, n_ctx, scan, tuple(jnp.zeros((64, 128), F32) for _ in range(per_dev))
    )
    lax.fori_loop(FIRST_PART, chunks * groups, second, 0)

    def take(s, _):
        copy2(me, lax.rem(me + s, n_ctx)).wait_recv()
        return 0

    lax.fori_loop(1, n_ctx, take, 0)

    ones = jnp.ones((8, 128), F32)

    def third(c, _):
        gate_copy(c).wait()
        r = pl.ds(pl.multiple_of(c * L, L), L)
        left = wide3(emask_s[c])
        skip3 = wide3(jnp.broadcast_to(skip_ref[...], (16, heads)))
        left = jnp.concatenate([left, skip3], axis=0)
        squares = jnp.zeros((L, 128), F32)
        for tile in range(x_hbm.shape[1] // TILE):
            lanes = slice(tile * TILE, (tile + 1) * TILE)
            g, at = divmod(tile * TILE, per_group * P_SIZE)
            here = slice(at, at + TILE)
            i = c * groups + g
            pieces = []
            for pair in (2 * tile, 2 * tile + 1):
                pieces.append(
                    jnp.concatenate(
                        [
                            recv2[k // per_dev, k % per_dev].astype(F32)
                            for k in (2 * pair, 2 * pair + 1)
                        ],
                        axis=0,
                    )
                )
            incoming = jnp.concatenate(pieces, axis=1)
            full = prefix[i, :, here] + pcar[c, 0:1, lanes] * incoming
            inter = dot(cconv[i], full.astype(BF16))
            spread = dot(left, sel[:, lanes])
            y = (
                yint[i, :, here]
                + spread[0:L] * inter
                + spread[L : L + 1] * xconv[i, :, here].astype(F32)
            )
            gated = y * silu(gate_buf[r, lanes].astype(F32))
            gate_buf[r, lanes] = gated.astype(BF16)
            sq = gated * gated
            squares = squares + sq[:, 0:128] + sq[:, 128:256]
        total = lax.dot_general(
            ones, squares, (((1,), (1,)), ((), ())), precision=HI, preferred_element_type=F32
        )
        sums[c] = total
        pltpu.make_async_copy(gate_buf.at[r, :], gated_hbm.at[r, :], out_sem.at[c]).start()
        return 0

    lax.fori_loop(0, chunks, third, 0)

    def sum_copy(other, slot):
        return pltpu.make_async_remote_copy(
            src_ref=sums,
            dst_ref=sums_recv.at[slot],
            send_sem=sum_ssem.at[other],
            recv_sem=sum_rsem.at[slot],
            device_id={"head": other},
            device_id_type=MESH,
        )

    def send_sum(s, _):
        sum_copy(lax.rem(my_head + s, n_head), my_head).start()
        return 0

    lax.fori_loop(1, n_head, send_sum, 0)

    def wait_out(c, _):
        r = pl.ds(pl.multiple_of(c * L, L), L)
        pltpu.make_async_copy(gate_buf.at[r, :], gated_hbm.at[r, :], out_sem.at[c]).wait()
        return 0

    def wait_sends(s, _):
        other = lax.rem(me + s, n_ctx)
        copy1(other, me).wait_send()
        copy2(other, me).wait_send()
        return 0

    lax.fori_loop(1, n_ctx, wait_sends, 0)
    for i in range(3):
        halo(i).wait_send()
    sums_recv[my_head] = sums[...]

    def take_sum(s, _):
        sum_copy(my_head, lax.rem(my_head + s, n_head)).wait_recv()
        return 0

    lax.fori_loop(1, n_head, take_sum, 0)
    total = sums_recv[0, :, 0, :]
    for k in range(1, n_head):
        total = total + sums_recv[k, :, 0, :]
    columns = n_head * heads * P_SIZE
    scale_ref[...] = lax.rsqrt(total / columns + EPS)

    def wait_sum(s, _):
        sum_copy(lax.rem(my_head + s, n_head), my_head).wait_send()
        return 0

    lax.fori_loop(1, n_head, wait_sum, 0)
    lax.fori_loop(0, chunks, wait_out, 0)


def solution(mesh):
    n_ctx = mesh.shape["ctx"]
    n_head = mesh.shape["head"]

    def shards(
        x_in, b_in, c_in, conv_x, conv_b, conv_c, step_size, decay_rate, skip, gate, norm_gain, doc_starts
    ):
        rows, cols = x_in.shape
        heads = step_size.shape[1]
        groups = b_in.shape[1] // N
        chunks = rows // L
        per_dev = PIECES // n_ctx
        wide = cols // groups
        per_group = heads // groups
        any_spec = pl.BlockSpec(memory_space=pl.ANY)
        vmem = pl.BlockSpec(memory_space=pltpu.VMEM)
        gated, scale = pl.pallas_call(
            functools.partial(kernel, n_ctx, n_head, chunks),
            out_shape=(
                jax.ShapeDtypeStruct((rows, cols), BF16),
                jax.ShapeDtypeStruct((chunks, L), F32),
            ),
            in_specs=[any_spec] * 4
            + [vmem] * 6
            + [pl.BlockSpec(memory_space=pltpu.SMEM)],
            out_specs=(any_spec, vmem),
            scratch_shapes=[
                pltpu.VMEM((rows + L, cols), BF16),
                pltpu.VMEM((2, rows + L, groups * N), BF16),
                pltpu.VMEM((rows, cols), BF16),
                pltpu.VMEM((chunks * groups, L, wide), BF16),
                pltpu.VMEM((chunks * groups, L, N), BF16),
                pltpu.VMEM((chunks * groups, L, N), BF16),
                pltpu.VMEM((chunks * groups, L, wide), F32),
                pltpu.VMEM((chunks * groups, N, wide), F32),
                pltpu.VMEM((groups, N, wide), F32),
                pltpu.VMEM((chunks + 1, 8, cols), F32),
                pltpu.VMEM((chunks * groups, L, per_group), F32),
                pltpu.VMEM((chunks * groups, per_group, L), F32),
                pltpu.VMEM((chunks, L, L), F32),
                pltpu.VMEM((chunks, L, heads), F32),
                pltpu.VMEM((3 * heads, cols), BF16),
                pltpu.VMEM((K - 1, 2, L, L), F32),
                pltpu.VMEM((L, L), F32),
                pltpu.VMEM((n_ctx, per_dev, ROWS, 128), BF16),
                pltpu.VMEM((n_ctx, per_dev, ROWS, 128), BF16),
                pltpu.VMEM((n_ctx, per_dev, 64, 128), BF16),
                pltpu.VMEM((n_ctx, per_dev, 64, 128), BF16),
                pltpu.VMEM((chunks, 8, L), F32),
                pltpu.VMEM((n_head, chunks, 8, L), F32),
                pltpu.SemaphoreType.DMA((chunks,)),
                pltpu.SemaphoreType.DMA((2,)),
                pltpu.SemaphoreType.DMA((chunks,)),
                pltpu.SemaphoreType.DMA((chunks,)),
                pltpu.SemaphoreType.DMA((3,)),
                pltpu.SemaphoreType.DMA((3,)),
                pltpu.SemaphoreType.DMA((n_ctx,)),
                pltpu.SemaphoreType.DMA((n_ctx,)),
                pltpu.SemaphoreType.DMA((n_ctx,)),
                pltpu.SemaphoreType.DMA((n_ctx,)),
                pltpu.SemaphoreType.DMA((n_head,)),
                pltpu.SemaphoreType.DMA((n_head,)),
            ],
            compiler_params=pltpu.CompilerParams(
                collective_id=0, has_side_effects=True, vmem_limit_bytes=62 * 1024 * 1024
            ),
        )(
            x_in,
            b_in,
            c_in,
            gate,
            conv_x,
            conv_b,
            conv_c,
            step_size,
            decay_rate.reshape(1, -1),
            skip.reshape(1, -1),
            doc_starts,
        )
        return (
            gated.astype(F32) * scale.reshape(rows, 1) * norm_gain.astype(F32)[None, :]
        ).astype(BF16)

    split = P("ctx", "head")
    taps = P(None, "head")
    line = P("head")
    return jax.shard_map(
        shards,
        mesh=mesh,
        in_specs=(split,) * 3 + (taps,) * 3 + (split, line, line, split, line, P()),
        out_specs=split,
        check_vma=False,
    )
```

time: 1150 us -> 95 us (0.08)
  the two profiles are of different devices: /device:TPU:24 before, /device:TPU:1 now
where the time goes in v1:
time: 95 us; the launch traced here: 94.8 us
  Pallas kernels  85.1 us (90%)
  other arithmetic  7.66 us (8%)
  local copies, waits for them, and re-layouts  2.08 us (2%)
    pallas_call x1, Pallas kernels, shards(): pl.pallas_call(functools.partial(kernel, n_ctx, n_head, chunks), out_shap...  85.1 us
    convert_element_type x1, other arithmetic, shards(): return (gated.astype(F32) * scale.reshape(rows, 1) * norm_gain.astype(F32...  6.98 us
    unnamed x1, local copies, waits for them, and re-layouts  2.08 us

profile of v1, /device:TPU:1, one launch (start us, length us, event | category | flops | bytes accessed | tf_op | source)
XLA Modules:
  0.0 94.8 jit_solution(7525725910437395263)
XLA Ops:
  0.0 0.7 convert_element_type.10
  0.7 2.1 %copy.13.step_ref = f32[1536,32]{1,0:T(8,128)} copy(f32[1536,32]{0,1:T(8,128)} %param.18) | data formatting | bytes 393216 | tf_op args[6]
  2.8 85.1 %shard_map.118 = (bf16[1536,2048]{1,0:T(8,128)(2,1)}, f32[12,128]{1,0:T(8,128)}) custom-call(bf16[1536,2048]{1,0:T(8,128)(2,1)} %x_hbm.1, bf16[1536,256]{1,0:T(8,128)(2,1)} %b_hbm.1, bf16[1536,256]{1,0:T(8,128)(2,1)} %c_hbm.1, bf16[1536,2048]{1,0:T(8,128)(2,1)} %gate_hbm.1, bf16[4,2048]{1,0:T(4,128)(2,1)} %taps_x.1, bf16[4,256]{1,0:T(4,128)(2,1)} %taps_b.1, ...), custom_call_target="tpu_custom_call" | custom-call | tf_op jit(solution)/shard_map/pallas_call | solution.py:499
  87.8 7.0 %multiply_convert_fusion = bf16[1536,2048]{1,0:T(8,128)(2,1)} fusion(bf16[1536,2048]{1,0:T(8,128)(2,1)} %get-tuple-element.7, f32[2048]{0:T(1024)S(1)} %convert_element_type.10, f32[1536]{0:T(1024)} %bitcast.3), kind=kLoop, calls=%fused_computation | loop fusion | flops 12582912 | bytes 12597248 | tf_op jit(solution)/shard_map/convert_element_type | solution.py:564

commit v2 on v1

v2 whole, which is shorter than its diff:
```python
import functools
import math

import jax
import jax.numpy as jnp
from jax import lax
from jax.experimental import pallas as pl
from jax.experimental.pallas import tpu as pltpu
from jax.sharding import PartitionSpec as P

F32 = jnp.float32
BF16 = jnp.bfloat16
P_SIZE = 64
N = 128
K = 4
L = 128
TILE = 256
CONV_TILE = 128
EPS = 1e-05
LOG2E = math.log2(math.e)
HI = lax.Precision.HIGHEST
MESH = pl.DeviceIdType.MESH
PIECES = 32
ROWS = 80
FIRST_PART = 12


def split3(v):
    hi = v.astype(BF16)
    rest = v - hi.astype(F32)
    mid = rest.astype(BF16)
    low = (rest - mid.astype(F32)).astype(BF16)
    return hi, mid, low


def dot(a, b, **kw):
    return jnp.dot(a, b, preferred_element_type=F32, **kw)


def kernel(
    n_ctx,
    n_head,
    chunks,
    x_hbm,
    b_hbm,
    c_hbm,
    gate_hbm,
    taps_x,
    taps_b,
    taps_c,
    step_ref,
    rate_ref,
    skip_ref,
    gain_ref,
    doc_ref,
    gate_buf,
    xbuf,
    bcbuf,
    yint,
    xconv,
    cconv,
    prefix,
    state,
    pcar,
    cum_all,
    cum_s,
    cumt_s,
    allow_s,
    scores_s,
    keep_s,
    left_s,
    carries,
    factors,
    sel,
    send1,
    recv1,
    send2,
    recv2,
    squares_s,
    sums,
    sums_recv,
    x_sem,
    bc_sem,
    gate_sem,
    halo_ssem,
    halo_rsem,
    ssem1,
    rsem1,
    ssem2,
    rsem2,
    sum_ssem,
    sum_rsem,
):
    me = lax.axis_index("ctx")
    my_head = lax.axis_index("head")
    rows = chunks * L
    heads = step_ref.shape[0]
    per_dev = PIECES // n_ctx

    def x_copy(c):
        r = pl.ds(pl.multiple_of(c * L, L), L)
        d = pl.ds(pl.multiple_of(c * L + L, L), L)
        return pltpu.make_async_copy(x_hbm.at[r, :], xbuf.at[d, :], x_sem.at[c])

    gate_copy = pltpu.make_async_copy(gate_hbm, gate_buf, gate_sem)
    b_copy = pltpu.make_async_copy(b_hbm, bcbuf.at[0, pl.ds(L, rows), :], bc_sem.at[0])
    c_copy = pltpu.make_async_copy(c_hbm, bcbuf.at[1, pl.ds(L, rows), :], bc_sem.at[1])
    b_copy.start()
    c_copy.start()

    def start_x(c, _):
        x_copy(c).start()
        return 0

    lax.fori_loop(0, 2, start_x, 0)

    barrier = pltpu.get_barrier_semaphore()

    def greet_ctx(s, _):
        pl.semaphore_signal(
            barrier, inc=1, device_id={"ctx": lax.rem(me + s, n_ctx)}, device_id_type=MESH
        )
        return 0

    def greet_head(s, _):
        pl.semaphore_signal(
            barrier, inc=1, device_id={"head": lax.rem(my_head + s, n_head)}, device_id_type=MESH
        )
        return 0

    lax.fori_loop(1, n_ctx, greet_ctx, 0)
    lax.fori_loop(1, n_head, greet_head, 0)

    sel_row = lax.broadcasted_iota(jnp.int32, (L, x_hbm.shape[1]), 0)
    sel_lane = lax.broadcasted_iota(jnp.int32, (L, x_hbm.shape[1]), 1)
    chosen = jnp.where(lax.rem(sel_row, heads) == lax.div(sel_lane, P_SIZE), 1.0, 0.0)
    sel[0] = jnp.where(sel_row < 2 * heads, chosen, 0.0).astype(BF16)
    sel[1] = jnp.where(sel_row >= 2 * heads, chosen, 0.0).astype(BF16)
    sel[2] = jnp.where(sel_row < 3 * heads, chosen, 0.0).astype(BF16)
    t_iota = lax.broadcasted_iota(jnp.int32, (L, L), 0)
    q_iota = lax.broadcasted_iota(jnp.int32, (L, L), 1)
    xbuf[0 : L - 16, :] = jnp.zeros((L - 16, xbuf.shape[1]), BF16)
    bcbuf[:, 0 : L - 16, :] = jnp.zeros((2, L - 16, bcbuf.shape[2]), BF16)
    state[...] = jnp.zeros_like(state)
    sums[...] = jnp.zeros_like(sums)
    groups = cconv.shape[0] // chunks
    per_group = heads // groups
    docs = [doc_ref[d] for d in range(doc_ref.shape[0])]

    def seg(pos):
        total = jnp.where(pos >= docs[0], 1, 0)
        for d in docs[1:]:
            total = total + jnp.where(pos >= d, 1, 0)
        return total

    pl.semaphore_wait(barrier, n_ctx + n_head - 2)

    rim = pl.ds(rows - 16, 16)
    spot = pl.ds(L - 16, 16)

    def halo(i):
        src = (x_hbm, b_hbm, c_hbm)[i].at[rim, :]
        dst = xbuf.at[spot, :] if i == 0 else bcbuf.at[i - 1, spot, :]
        return pltpu.make_async_remote_copy(
            src_ref=src,
            dst_ref=dst,
            send_sem=halo_ssem.at[i],
            recv_sem=halo_rsem.at[i],
            device_id={"ctx": lax.rem(me + 1, n_ctx)},
            device_id_type=MESH,
        )

    for i in range(3):
        halo(i).start()

    lax.fori_loop(2, chunks, start_x, 0)

    gate_copy.start()

    eye = lax.broadcasted_iota(jnp.int32, (heads, heads), 0) == lax.broadcasted_iota(
        jnp.int32, (heads, heads), 1
    )

    def column(row):
        return jnp.sum(
            jnp.where(eye, jnp.broadcast_to(row, (heads, heads)), 0.0), axis=1, keepdims=True
        )

    rate = column(rate_ref[...]) * -LOG2E
    steps = [step_ref[:, c * L : (c + 1) * L] for c in range(chunks)]
    triu = jnp.where(t_iota <= q_iota, 1.0, 0.0)
    cum_all[...] = dot(jnp.concatenate([v * rate for v in steps], axis=0), triu, precision=HI)
    carries[...] = jnp.where(
        lax.broadcasted_iota(jnp.int32, (heads, L), 1) == chunks, column(skip_ref[...]), 0.0
    )

    def decays(c, _):
        base = me * rows + c * L
        here = pl.ds(pl.multiple_of(c * heads, heads), heads)
        cum = cum_all[here, :]
        step = step_ref[:, pl.ds(pl.multiple_of(c * L, L), L)]
        cum_j = cum - jnp.log(step) * LOG2E
        h_lane = lax.broadcasted_iota(jnp.int32, (heads, L), 1)
        seg_j = seg(base + h_lane)
        seg_last = seg(base + L - 1)
        seg_before = seg(base - 1)
        last = cum[:, L - 1 : L]
        weight = jnp.where(seg_j == seg_last, jnp.exp2(last - cum_j), 0.0)
        inflow = jnp.where(seg_j == seg_before, jnp.exp2(cum), 0.0)
        carry = jnp.where(seg_last == seg_before, jnp.exp2(last), 0.0)
        carries[...] = jnp.where(h_lane == c, carry, carries[...])
        w_hi = weight.astype(BF16).astype(F32)
        i_hi = inflow.astype(BF16).astype(F32)
        stack = jnp.concatenate([w_hi, weight - w_hi, i_hi, inflow - i_hi], axis=0)
        left_s[c] = stack.T.astype(BF16)
        cum_t = jnp.concatenate([cum, jnp.zeros((L - heads, L), F32)], axis=0).T
        for g in range(groups):
            hs = slice(g * per_group, (g + 1) * per_group)
            cum_s[c * groups + g] = cum_t[:, hs]
            cumt_s[c * groups + g] = cum_j[hs, :]
        seg_t = seg(base + t_iota)
        seg_q = seg(base + lax.broadcasted_iota(jnp.int32, (1, L), 1))
        allow_s[c] = jnp.where(jnp.logical_and(seg_t == seg_q, t_iota >= q_iota), 1.0, 0.0)
        since = jnp.full((L, L), 4, jnp.int32)
        for d in docs:
            gap = base + t_iota - d
            since = jnp.minimum(since, jnp.where(gap < 0, 4, gap))
        for s in range(1, K):
            keep_s[c, s - 1] = jnp.where(since < s, 0.0, 1.0)
        return 0

    lax.fori_loop(0, chunks, decays, 0)
    c_hi, c_mid, c_low = split3(carries[...])
    c_all = jnp.concatenate(
        [v.astype(F32) for v in (c_hi, c_mid, c_low)] + [jnp.zeros((L - 3 * heads, L), F32)], axis=0
    )
    factors[...] = dot(c_all.T.astype(BF16)[0:16, :], sel[2])

    b_copy.wait()
    c_copy.wait()
    for i in range(3):
        halo(i).wait_recv()

    def conv(win, taps, keep):
        w = win.astype(F32)
        half = taps * 0.5
        v = (pltpu.roll(w, 3, 0)[16:] * keep[2]) * half[0:1]
        v = v + (pltpu.roll(w, 2, 0)[16:] * keep[1]) * half[1:2]
        v = v + (pltpu.roll(w, 1, 0)[16:] * keep[0]) * half[2:3]
        v = v + w[16:] * half[3:4]
        return v + v * jnp.tanh(v)

    def first(c, _, w=True):
        if w:
            x_copy(c).wait()
        window = pl.ds(pl.multiple_of(c * L + L - 16, 16), L + 16)
        keep = [keep_s[c, s] for s in range(K - 1)]
        left = left_s[c]
        b_t = []
        for g in range(groups):
            lanes = slice(g * N, (g + 1) * N)
            b_now = conv(bcbuf[0, window, lanes], taps_b[:, lanes].astype(F32), keep)
            b_t.append(b_now.T.astype(BF16))
            c_now = conv(bcbuf[1, window, lanes], taps_c[:, lanes].astype(F32), keep).astype(BF16)
            cconv[c * groups + g] = c_now
            scores_s[c * groups + g] = allow_s[c] * dot(c_now, b_t[g])
        for tile in range(x_hbm.shape[1] // TILE):
            lanes = slice(tile * TILE, (tile + 1) * TILE)
            g, at = divmod(tile * TILE, per_group * P_SIZE)
            here = slice(at, at + TILE)
            spread = dot(left, sel[0, :, lanes])
            parts = []
            for half in range(TILE // 128):
                sub = slice(tile * TILE + half * 128, tile * TILE + (half + 1) * 128)
                x_now = conv(xbuf[window, sub], taps_x[:, sub].astype(F32), keep).astype(BF16)
                xconv[c * groups + g, :, at + half * 128 : at + (half + 1) * 128] = x_now
                parts.append(
                    (x_now.astype(F32) * spread[:, half * 128 : (half + 1) * 128]).astype(BF16)
                )
            local = dot(b_t[g], jnp.concatenate(parts, axis=1))
            factor = factors[pl.ds(c, 1), lanes]
            before = state[g, :, here]
            prefix[c * groups + g, :, here] = before
            state[g, :, here] = before * factor + local
            old = jnp.where(c == 0, 1.0, pcar[c, 0:1, lanes])
            pcar[c, 0:1, lanes] = old
            pcar[c + 1, 0:1, lanes] = old * factor
        return 0

    lax.fori_loop(0, chunks, first, 0)

    r_iota = lax.broadcasted_iota(jnp.int32, (16, 128), 0)
    for pair in range(PIECES // 2):
        g, at = divmod(pair * 128, per_group * P_SIZE)
        hi, mid, low = split3(
            jnp.broadcast_to(pcar[chunks, 0:1, pair * 128 : (pair + 1) * 128], (16, 128))
        )
        tail = jnp.where(
            r_iota == 0,
            hi.astype(F32),
            jnp.where(r_iota == 1, mid.astype(F32), jnp.where(r_iota == 2, low.astype(F32), 0.0)),
        ).astype(BF16)
        for half in range(2):
            k = pair * 2 + half
            send1[k // per_dev, k % per_dev, 0:64, :] = state[
                g, half * 64 : (half + 1) * 64, at : at + 128
            ].astype(BF16)
            send1[k // per_dev, k % per_dev, 64:80, :] = tail

    def copy1(other):
        return pltpu.make_async_remote_copy(
            src_ref=send1.at[other],
            dst_ref=recv1.at[me],
            send_sem=ssem1,
            recv_sem=rsem1,
            device_id={"ctx": other},
            device_id_type=MESH,
        )

    def copy2(other):
        return pltpu.make_async_remote_copy(
            src_ref=send2.at[other],
            dst_ref=recv2.at[me],
            send_sem=ssem2,
            recv_sem=rsem2,
            device_id={"ctx": other},
            device_id_type=MESH,
        )

    def all_of(send, recv, ssem, rsem):
        some = pl.ds(0, n_ctx - 1)
        return pltpu.make_async_remote_copy(
            src_ref=send.at[some],
            dst_ref=recv.at[some],
            send_sem=ssem,
            recv_sem=rsem,
            device_id={"ctx": lax.rem(me + 1, n_ctx)},
            device_id_type=MESH,
        )

    all1 = all_of(send1, recv1, ssem1, rsem1)
    all2 = all_of(send2, recv2, ssem2, rsem2)

    def send_state(s, _):
        copy1(lax.rem(me + s, n_ctx)).start()
        return 0

    lax.fori_loop(1, n_ctx, send_state, 0)
    recv1[me] = send1[me]

    lane = lax.broadcasted_iota(jnp.int32, (L, 128), 1)

    def second(i, _):
        c = lax.div(i, groups)
        scores = scores_s[i]
        cum = cum_s[i]
        for pair in range(per_group // 2):
            ws = []
            for h in (2 * pair, 2 * pair + 1):
                gap = cum[:, h : h + 1] - cumt_s[i, h : h + 1, :]
                ws.append((scores * jnp.exp2(jnp.minimum(gap, 4.0))).astype(BF16))
            x_pair = xconv[i, :, pair * 128 : (pair + 1) * 128]
            zero = jnp.zeros_like(x_pair)
            both = jnp.concatenate(
                [jnp.where(lane < P_SIZE, x_pair, zero), jnp.where(lane < P_SIZE, zero, x_pair)],
                axis=0,
            )
            yint[i, :, pair * 128 : (pair + 1) * 128] = dot(jnp.concatenate(ws, axis=1), both)
        return 0

    lax.fori_loop(0, FIRST_PART, second, 0, unroll=4)

    all1.wait_recv()

    def scan(e, acc):
        out = []
        for k in range(per_dev):
            send2[e, k] = acc[k].astype(BF16)
            got = recv1[e, k].astype(F32)
            factor = got[64:65] + got[65:66] + got[66:67]
            out.append(acc[k] * factor + got[0:64])
        return tuple(out)

    lax.fori_loop(
        0, n_ctx, scan, tuple(jnp.zeros((64, 128), F32) for _ in range(per_dev)), unroll=4
    )

    def send_back(s, _):
        copy2(lax.rem(me + s, n_ctx)).start()
        return 0

    lax.fori_loop(1, n_ctx, send_back, 0)
    recv2[me] = send2[me]
    lax.fori_loop(FIRST_PART, chunks * groups, second, 0, unroll=4)

    all2.wait_recv()

    def sum_copy(part, other):
        some = pl.ds(part * 8, 8)
        return pltpu.make_async_remote_copy(
            src_ref=sums.at[some, :],
            dst_ref=sums_recv.at[my_head, some, :],
            send_sem=sum_ssem.at[part],
            recv_sem=sum_rsem.at[part],
            device_id={"head": other},
            device_id_type=MESH,
        )

    def sums_in(part):
        some = pl.ds(part * 8, 8)
        whole = sums_recv.at[pl.ds(0, n_head - 1), some, :]
        return pltpu.make_async_remote_copy(
            src_ref=whole,
            dst_ref=whole,
            send_sem=sum_ssem.at[part],
            recv_sem=sum_rsem.at[part],
            device_id={"head": lax.rem(my_head + 1, n_head)},
            device_id_type=MESH,
        )

    def send_sums(part):
        for s in range(1, n_head):
            sum_copy(part, lax.rem(my_head + s, n_head)).start()
        some = slice(part * 8, part * 8 + 8)
        sums_recv[my_head, some, :] = sums[some, :]

    def add_up(c):
        total = jnp.sum(squares_s[lax.rem(c, 2)].T, axis=0, keepdims=True)
        sums[pl.ds(c, 1), :] = total

    def third(c, _, w=True, skip_sum=False):
        if not skip_sum:
            add_up(c - 1)
        r = pl.ds(pl.multiple_of(c * L, L), L)
        squares = jnp.zeros((L, 128), F32)
        for tile in range(x_hbm.shape[1] // TILE):
            lanes = slice(tile * TILE, (tile + 1) * TILE)
            g, at = divmod(tile * TILE, per_group * P_SIZE)
            here = slice(at, at + TILE)
            i = c * groups + g
            pieces = []
            for pair in (2 * tile, 2 * tile + 1):
                pieces.append(
                    jnp.concatenate(
                        [
                            recv2[k // per_dev, k % per_dev].astype(F32)
                            for k in (2 * pair, 2 * pair + 1)
                        ],
                        axis=0,
                    )
                )
            incoming = jnp.concatenate(pieces, axis=1)
            full = prefix[i, :, here] + pcar[c, 0:1, lanes] * incoming
            inter = dot(cconv[i], full.astype(BF16))
            spread = dot(left_s[c], sel[1, :, lanes])
            y = (
                yint[i, :, here]
                + spread * inter
                + factors[chunks : chunks + 1, lanes] * xconv[i, :, here].astype(F32)
            )
            v = gate_buf[r, lanes].astype(F32) * 0.5
            gated = y * (v + v * jnp.tanh(v))
            yint[i, :, here] = gated
            sq = gated * gated
            squares = squares + sq[:, 0:128] + sq[:, 128:256]
        squares_s[lax.rem(c, 2)] = squares
        return 0

    gate_copy.wait()
    third(0, 0, skip_sum=True)
    lax.fori_loop(1, 9, third, 0)
    send_sums(0)
    lax.fori_loop(9, chunks, third, 0)
    add_up(chunks - 1)
    send_sums(1)

    all1.wait_send()
    all2.wait_send()
    for i in range(3):
        halo(i).wait_send()

    columns = n_head * heads * P_SIZE

    def norm(c, _):
        total = sums_recv[0, pl.ds(c, 1), :]
        for k in range(1, n_head):
            total = total + sums_recv[k, pl.ds(c, 1), :]
        row = lax.rsqrt(total / columns + EPS)
        scale = jnp.broadcast_to(row, (L, L)).T
        r = pl.ds(pl.multiple_of(c * L, L), L)
        for at in range(0, x_hbm.shape[1], L):
            g, off = divmod(at, per_group * P_SIZE)
            gain = gain_ref[at : at + L].astype(F32)[None, :]
            value = yint[c * groups + g, :, off : off + L] * scale * gain
            gate_buf[r, at : at + L] = value.astype(BF16)
        return 0

    sums_in(0).wait_recv()
    lax.fori_loop(0, 8, norm, 0)
    sums_in(1).wait_recv()
    lax.fori_loop(8, chunks, norm, 0)
    sums_in(0).wait_send()
    sums_in(1).wait_send()


def store(chunks, from_ref, out_hbm, sem):
    def copy(c):
        r = pl.ds(pl.multiple_of(c * L, L), L)
        return pltpu.make_async_copy(from_ref.at[r, :], out_hbm.at[r, :], sem.at[c])

    def begin(c, _):
        copy(c).start()
        return 0

    def finish(c, _):
        copy(c).wait()
        return 0

    lax.fori_loop(0, chunks, begin, 0)
    lax.fori_loop(0, chunks, finish, 0)


def solution(mesh):
    n_ctx = mesh.shape["ctx"]
    n_head = mesh.shape["head"]

    def shards(
        x_in, b_in, c_in, conv_x, conv_b, conv_c, step_size, decay_rate, skip, gate, norm_gain, doc_starts
    ):
        rows, cols = x_in.shape
        heads = step_size.shape[1]
        groups = b_in.shape[1] // N
        chunks = rows // L
        per_dev = PIECES // n_ctx
        wide = cols // groups
        per_group = heads // groups
        any_spec = pl.BlockSpec(memory_space=pl.ANY)
        vmem = pl.BlockSpec(memory_space=pltpu.VMEM)
        mixed = pl.pallas_call(
            functools.partial(kernel, n_ctx, n_head, chunks),
            out_shape=pltpu.VMEM((rows, cols), BF16),
            in_specs=[any_spec] * 4
            + [vmem] * 7
            + [pl.BlockSpec(memory_space=pltpu.SMEM)],
            out_specs=vmem,
            scratch_shapes=[
                pltpu.VMEM((rows + L, cols), BF16),
                pltpu.VMEM((2, rows + L, groups * N), BF16),
                pltpu.VMEM((chunks * groups, L, wide), F32),
                pltpu.VMEM((chunks * groups, L, wide), BF16),
                pltpu.VMEM((chunks * groups, L, N), BF16),
                pltpu.VMEM((chunks * groups, N, wide), F32),
                pltpu.VMEM((groups, N, wide), F32),
                pltpu.VMEM((chunks + 1, 8, cols), F32),
                pltpu.VMEM((chunks * heads, L), F32),
                pltpu.VMEM((chunks * groups, L, per_group), F32),
                pltpu.VMEM((chunks * groups, per_group, L), F32),
                pltpu.VMEM((chunks, L, L), F32),
                pltpu.VMEM((chunks * groups, L, L), F32),
                pltpu.VMEM((chunks, K - 1, L, L), F32),
                pltpu.VMEM((chunks, L, L), BF16),
                pltpu.VMEM((heads, L), F32),
                pltpu.VMEM((16, cols), F32),
                pltpu.VMEM((3, L, cols), BF16),
                pltpu.VMEM((n_ctx, per_dev, ROWS, 128), BF16),
                pltpu.VMEM((n_ctx, per_dev, ROWS, 128), BF16),
                pltpu.VMEM((n_ctx, per_dev, 64, 128), BF16),
                pltpu.VMEM((n_ctx, per_dev, 64, 128), BF16),
                pltpu.VMEM((2, L, 128), F32),
                pltpu.VMEM((16, L), F32),
                pltpu.VMEM((n_head, 16, L), F32),
                pltpu.SemaphoreType.DMA((chunks,)),
                pltpu.SemaphoreType.DMA((2,)),
                pltpu.SemaphoreType.DMA,
                pltpu.SemaphoreType.DMA((3,)),
                pltpu.SemaphoreType.DMA((3,)),
                pltpu.SemaphoreType.DMA,
                pltpu.SemaphoreType.DMA,
                pltpu.SemaphoreType.DMA,
                pltpu.SemaphoreType.DMA,
                pltpu.SemaphoreType.DMA((2,)),
                pltpu.SemaphoreType.DMA((2,)),
            ],
            compiler_params=pltpu.CompilerParams(
                collective_id=0, has_side_effects=True, vmem_limit_bytes=56 * 1024 * 1024
            ),
        )(
            x_in,
            b_in,
            c_in,
            gate,
            conv_x,
            conv_b,
            conv_c,
            step_size.T,
            decay_rate.reshape(1, -1),
            skip.reshape(1, -1),
            norm_gain,
            doc_starts,
        )
        return pl.pallas_call(
            functools.partial(store, chunks),
            out_shape=jax.ShapeDtypeStruct((rows, cols), BF16),
            in_specs=[vmem],
            out_specs=any_spec,
            scratch_shapes=[pltpu.SemaphoreType.DMA((chunks,))],
            compiler_params=pltpu.CompilerParams(vmem_limit_bytes=24 * 1024 * 1024),
        )(mixed)

    split = P("ctx", "head")
    taps = P(None, "head")
    line = P("head")
    return jax.shard_map(
        shards,
        mesh=mesh,
        in_specs=(split,) * 3 + (taps,) * 3 + (split, line, line, split, line, P()),
        out_specs=split,
        check_vma=False,
    )
```

time: 95 us -> 65.3 us (0.69)
  Pallas kernels: 85.1 us -> 65.1 us
  other arithmetic: 7.66 us -> 0 us
  local copies, waits for them, and re-layouts: 2.08 us -> 0 us
    pallas_call x1, Pallas kernels: 85.1 us -> 62.4 us  [shards(): pl.pallas_call(functools.partial(kernel, n_ctx, n_head, chunks), out_shap...]
    convert_element_type x2 -> x0, other arithmetic: 7.66 us -> none  [the longest x1 6.98 us: shards(): return (gated.astype(F32) * scale.reshape(rows, 1) * norm_gain.astype(F32...]
    pallas_call x0 -> x1, Pallas kernels: none -> 2.75 us  [shards(): pl.pallas_call(functools.partial(store, chunks), out_shape=jax.ShapeDtype...]
    unnamed x1 -> x0, local copies, waits for them, and re-layouts: 2.08 us -> none
where the time goes in v2:
time: 65.3 us; the launch traced here: 65.2 us
  Pallas kernels  65.1 us (100%)
    pallas_call x1, Pallas kernels, shards(): pl.pallas_call(functools.partial(kernel, n_ctx, n_head, chunks), out_shap...  62.4 us
    pallas_call x1, Pallas kernels, shards(): pl.pallas_call(functools.partial(store, chunks), out_shape=jax.ShapeDtype...  2.75 us

profile of v2, /device:TPU:1, one launch (start us, length us, event | category | flops | bytes accessed | tf_op | source)
XLA Modules:
  0.0 65.2 jit_solution(2199347600456057534)
XLA Ops:
  0.0 62.4 %shard_map.118.from_ref = bf16[1536,2048]{1,0:T(8,128)(2,1)S(1)} custom-call(bf16[1536,2048]{1,0:T(8,128)(2,1)} %x_hbm.1, bf16[1536,256]{1,0:T(8,128)(2,1)} %b_hbm.1, bf16[1536,256]{1,0:T(8,128)(2,1)} %c_hbm.1, bf16[1536,2048]{1,0:T(8,128)(2,1)} %gate_hbm.1, bf16[4,2048]{1,0:T(4,128)(2,1)} %taps_x.1, bf16[4,256]{1,0:T(4,128)(2,1)} %taps_b.1, ...), custom_call_target="tpu_custom_call" | custom-call | tf_op jit(solution)/shard_map/pallas_call | solution.py:539
  62.4 2.8 %shard_map.119 = bf16[1536,2048]{1,0:T(8,128)(2,1)} custom-call(bf16[1536,2048]{1,0:T(8,128)(2,1)S(1)} %shard_map.118.from_ref), custom_call_target="tpu_custom_call" | custom-call | tf_op jit(solution)/shard_map/pallas_call | solution.py:601

commit v3 on v2

--- a/solution.py
+++ b/solution.py
@@ -13,6 +13,7 @@
 P_SIZE = 64
 N = 128
 K = 4
+RIM = 16
 L = 128
 TILE = 256
 CONV_TILE = 128
@@ -20,9 +21,9 @@
 LOG2E = math.log2(math.e)
 HI = lax.Precision.HIGHEST
 MESH = pl.DeviceIdType.MESH
-PIECES = 32
+PIECES = 16
 ROWS = 80
-FIRST_PART = 12
+FIRST_PART = 24
 
 
 def split3(v):
@@ -54,6 +55,7 @@
     gain_ref,
     doc_ref,
     gate_buf,
+    conv_s,
     xbuf,
     bcbuf,
     yint,
@@ -61,6 +63,7 @@
     cconv,
     prefix,
     state,
+    start_s,
     pcar,
     cum_all,
     cum_s,
@@ -95,16 +98,18 @@
     my_head = lax.axis_index("head")
     rows = chunks * L
     heads = step_ref.shape[0]
-    per_dev = PIECES // n_ctx
+    owners = max(n_ctx // 2, 1)
+    per_dev = PIECES // owners
+    split = n_ctx == 32
 
     def x_copy(c):
         r = pl.ds(pl.multiple_of(c * L, L), L)
-        d = pl.ds(pl.multiple_of(c * L + L, L), L)
+        d = pl.ds(pl.multiple_of(c * L + RIM, RIM), L)
         return pltpu.make_async_copy(x_hbm.at[r, :], xbuf.at[d, :], x_sem.at[c])
 
     gate_copy = pltpu.make_async_copy(gate_hbm, gate_buf, gate_sem)
-    b_copy = pltpu.make_async_copy(b_hbm, bcbuf.at[0, pl.ds(L, rows), :], bc_sem.at[0])
-    c_copy = pltpu.make_async_copy(c_hbm, bcbuf.at[1, pl.ds(L, rows), :], bc_sem.at[1])
+    b_copy = pltpu.make_async_copy(b_hbm, bcbuf.at[0, pl.ds(RIM, rows), :], bc_sem.at[0])
+    c_copy = pltpu.make_async_copy(c_hbm, bcbuf.at[1, pl.ds(RIM, rows), :], bc_sem.at[1])
     b_copy.start()
     c_copy.start()
 
@@ -112,7 +117,8 @@
         x_copy(c).start()
         return 0
 
-    lax.fori_loop(0, 2, start_x, 0)
+    lax.fori_loop(0, chunks, start_x, 0)
+    gate_copy.start()
 
     barrier = pltpu.get_barrier_semaphore()
 
@@ -139,8 +145,8 @@
     sel[2] = jnp.where(sel_row < 3 * heads, chosen, 0.0).astype(BF16)
     t_iota = lax.broadcasted_iota(jnp.int32, (L, L), 0)
     q_iota = lax.broadcasted_iota(jnp.int32, (L, L), 1)
-    xbuf[0 : L - 16, :] = jnp.zeros((L - 16, xbuf.shape[1]), BF16)
-    bcbuf[:, 0 : L - 16, :] = jnp.zeros((2, L - 16, bcbuf.shape[2]), BF16)
+    pcar[0, 0:1, :] = jnp.zeros((1, pcar.shape[2]), F32)
+    pcar[1, 0:1, :] = jnp.ones((1, pcar.shape[2]), F32)
     state[...] = jnp.zeros_like(state)
     sums[...] = jnp.zeros_like(sums)
     groups = cconv.shape[0] // chunks
@@ -152,30 +158,6 @@
         for d in docs[1:]:
             total = total + jnp.where(pos >= d, 1, 0)
         return total
-
-    pl.semaphore_wait(barrier, n_ctx + n_head - 2)
-
-    rim = pl.ds(rows - 16, 16)
-    spot = pl.ds(L - 16, 16)
-
-    def halo(i):
-        src = (x_hbm, b_hbm, c_hbm)[i].at[rim, :]
-        dst = xbuf.at[spot, :] if i == 0 else bcbuf.at[i - 1, spot, :]
-        return pltpu.make_async_remote_copy(
-            src_ref=src,
-            dst_ref=dst,
-            send_sem=halo_ssem.at[i],
-            recv_sem=halo_rsem.at[i],
-            device_id={"ctx": lax.rem(me + 1, n_ctx)},
-            device_id_type=MESH,
-        )
-
-    for i in range(3):
-        halo(i).start()
-
-    lax.fori_loop(2, chunks, start_x, 0)
-
-    gate_copy.start()
 
     eye = lax.broadcasted_iota(jnp.int32, (heads, heads), 0) == lax.broadcasted_iota(
         jnp.int32, (heads, heads), 1
@@ -229,124 +211,233 @@
             keep_s[c, s - 1] = jnp.where(since < s, 0.0, 1.0)
         return 0
 
-    lax.fori_loop(0, chunks, decays, 0)
+    lax.fori_loop(0, chunks, decays, 0, unroll=4)
     c_hi, c_mid, c_low = split3(carries[...])
     c_all = jnp.concatenate(
         [v.astype(F32) for v in (c_hi, c_mid, c_low)] + [jnp.zeros((L - 3 * heads, L), F32)], axis=0
     )
     factors[...] = dot(c_all.T.astype(BF16)[0:16, :], sel[2])
 
+    rim = pl.ds(rows - RIM, RIM)
+    spot = pl.ds(0, RIM)
+
+    def halo(i):
+        src = (x_hbm, b_hbm, c_hbm)[i].at[rim, :]
+        dst = xbuf.at[spot, :] if i == 0 else bcbuf.at[i - 1, spot, :]
+        return pltpu.make_async_remote_copy(
+            src_ref=src,
+            dst_ref=dst,
+            send_sem=halo_ssem.at[i],
+            recv_sem=halo_rsem.at[i],
+            device_id={"ctx": lax.rem(me + 1, n_ctx)},
+            device_id_type=MESH,
+        )
+
     b_copy.wait()
     c_copy.wait()
-    for i in range(3):
-        halo(i).wait_recv()
-
-    def conv(win, taps, keep):
+    x_copy(0).wait()
+
+    def conv(win, taps, keep, slot):
         w = win.astype(F32)
+        cs = conv_s.at[slot]
+        cs[...] = w
         half = taps * 0.5
-        v = (pltpu.roll(w, 3, 0)[16:] * keep[2]) * half[0:1]
-        v = v + (pltpu.roll(w, 2, 0)[16:] * keep[1]) * half[1:2]
-        v = v + (pltpu.roll(w, 1, 0)[16:] * keep[0]) * half[2:3]
+        v = (cs[13 : 13 + L, :] * keep[2]) * half[0:1]
+        v = v + (cs[14 : 14 + L, :] * keep[1]) * half[1:2]
+        v = v + (cs[15 : 15 + L, :] * keep[0]) * half[2:3]
         v = v + w[16:] * half[3:4]
         return v + v * jnp.tanh(v)
 
-    def first(c, _, w=True):
-        if w:
+    def first(g, w, c, _):
+        at_start = isinstance(c, int)
+        if w and not at_start:
             x_copy(c).wait()
-        window = pl.ds(pl.multiple_of(c * L + L - 16, 16), L + 16)
+        i = c * groups + g
+        window = pl.ds(pl.multiple_of(c * L, L), L + RIM)
         keep = [keep_s[c, s] for s in range(K - 1)]
         left = left_s[c]
-        b_t = []
-        for g in range(groups):
-            lanes = slice(g * N, (g + 1) * N)
-            b_now = conv(bcbuf[0, window, lanes], taps_b[:, lanes].astype(F32), keep)
-            b_t.append(b_now.T.astype(BF16))
-            c_now = conv(bcbuf[1, window, lanes], taps_c[:, lanes].astype(F32), keep).astype(BF16)
-            cconv[c * groups + g] = c_now
-            scores_s[c * groups + g] = allow_s[c] * dot(c_now, b_t[g])
-        for tile in range(x_hbm.shape[1] // TILE):
-            lanes = slice(tile * TILE, (tile + 1) * TILE)
-            g, at = divmod(tile * TILE, per_group * P_SIZE)
+        mine = slice(g * N, (g + 1) * N)
+        b_now = conv(bcbuf[0, window, mine], taps_b[:, mine].astype(F32), keep, 0)
+        b_t = b_now.T.astype(BF16)
+        c_now = conv(bcbuf[1, window, mine], taps_c[:, mine].astype(F32), keep, 1).astype(BF16)
+        cconv[i] = c_now
+        scores_s[i] = allow_s[c] * dot(c_now, b_t)
+        wide = per_group * P_SIZE
+        for at in range(0, wide, TILE):
+            lanes = slice(g * wide + at, g * wide + at + TILE)
             here = slice(at, at + TILE)
             spread = dot(left, sel[0, :, lanes])
             parts = []
-            for half in range(TILE // 128):
-                sub = slice(tile * TILE + half * 128, tile * TILE + (half + 1) * 128)
-                x_now = conv(xbuf[window, sub], taps_x[:, sub].astype(F32), keep).astype(BF16)
-                xconv[c * groups + g, :, at + half * 128 : at + (half + 1) * 128] = x_now
-                parts.append(
-                    (x_now.astype(F32) * spread[:, half * 128 : (half + 1) * 128]).astype(BF16)
-                )
-            local = dot(b_t[g], jnp.concatenate(parts, axis=1))
+            for half in range(0, TILE, 128):
+                sub = slice(lanes.start + half, lanes.start + half + 128)
+                x_now = conv(xbuf[window, sub], taps_x[:, sub].astype(F32), keep, 2 + (at + half) // 128).astype(BF16)
+                xconv[i, :, at + half : at + half + 128] = x_now
+                parts.append((x_now.astype(F32) * spread[:, half : half + 128]).astype(BF16))
+            local = dot(b_t, jnp.concatenate(parts, axis=1))
+            if at_start:
+                start_s[g, :, here] = local
+                continue
             factor = factors[pl.ds(c, 1), lanes]
             before = state[g, :, here]
-            prefix[c * groups + g, :, here] = before
+            prefix[i, :, here] = before
             state[g, :, here] = before * factor + local
-            old = jnp.where(c == 0, 1.0, pcar[c, 0:1, lanes])
-            pcar[c, 0:1, lanes] = old
-            pcar[c + 1, 0:1, lanes] = old * factor
-        return 0
-
-    lax.fori_loop(0, chunks, first, 0)
+            pcar[c + 1, 0:1, lanes] = pcar[c, 0:1, lanes] * factor
+        return 0
+
+    def owner(g, q):
+        if not split:
+            return q * min(n_ctx, 2) + (g if n_ctx > 1 else 0)
+        y, z_hi, x = lax.div(q, 4), lax.rem(lax.div(q, 2), 2), lax.rem(q, 2)
+        return (y * 4 + z_hi * 2 + lax.rem(y + g, 2)) * 2 + x
+
+    if split:
+        my_y, my_z = lax.div(me, 8), lax.rem(lax.div(me, 2), 4)
+        my_g = lax.rem(my_y + my_z, 2)
+        my_q = (my_y * 2 + lax.div(my_z, 2)) * 2 + lax.rem(me, 2)
+    else:
+        my_g, my_q = lax.rem(me, 2), lax.div(me, 2)
+
+    def owns(g):
+        return my_g == g if n_ctx > 1 else True
 
     r_iota = lax.broadcasted_iota(jnp.int32, (16, 128), 0)
-    for pair in range(PIECES // 2):
-        g, at = divmod(pair * 128, per_group * P_SIZE)
-        hi, mid, low = split3(
-            jnp.broadcast_to(pcar[chunks, 0:1, pair * 128 : (pair + 1) * 128], (16, 128))
-        )
-        tail = jnp.where(
-            r_iota == 0,
-            hi.astype(F32),
-            jnp.where(r_iota == 1, mid.astype(F32), jnp.where(r_iota == 2, low.astype(F32), 0.0)),
-        ).astype(BF16)
-        for half in range(2):
-            k = pair * 2 + half
-            send1[k // per_dev, k % per_dev, 0:64, :] = state[
-                g, half * 64 : (half + 1) * 64, at : at + 128
-            ].astype(BF16)
-            send1[k // per_dev, k % per_dev, 64:80, :] = tail
-
-    def copy1(other):
+
+    def copy1(g, q):
         return pltpu.make_async_remote_copy(
-            src_ref=send1.at[other],
+            src_ref=send1.at[g, q],
             dst_ref=recv1.at[me],
-            send_sem=ssem1,
+            send_sem=ssem1.at[g],
             recv_sem=rsem1,
+            device_id={"ctx": owner(g, q)},
+            device_id_type=MESH,
+        )
+
+    def copy2(g, other):
+        return pltpu.make_async_remote_copy(
+            src_ref=send2.at[other],
+            dst_ref=recv2.at[g, my_q],
+            send_sem=ssem2,
+            recv_sem=rsem2.at[g],
             device_id={"ctx": other},
             device_id_type=MESH,
         )
 
-    def copy2(other):
+    def bulk(ref, ssem, rsem):
         return pltpu.make_async_remote_copy(
-            src_ref=send2.at[other],
-            dst_ref=recv2.at[me],
-            send_sem=ssem2,
-            recv_sem=rsem2,
-            device_id={"ctx": other},
-            device_id_type=MESH,
-        )
-
-    def all_of(send, recv, ssem, rsem):
-        some = pl.ds(0, n_ctx - 1)
-        return pltpu.make_async_remote_copy(
-            src_ref=send.at[some],
-            dst_ref=recv.at[some],
+            src_ref=ref,
+            dst_ref=ref,
             send_sem=ssem,
             recv_sem=rsem,
             device_id={"ctx": lax.rem(me + 1, n_ctx)},
             device_id_type=MESH,
         )
 
-    all1 = all_of(send1, recv1, ssem1, rsem1)
-    all2 = all_of(send2, recv2, ssem2, rsem2)
-
-    def send_state(s, _):
-        copy1(lax.rem(me + s, n_ctx)).start()
-        return 0
-
-    lax.fori_loop(1, n_ctx, send_state, 0)
-    recv1[me] = send1[me]
+    def send_state(g):
+        for pair in range(PIECES // 2):
+            here = slice(pair * 128, pair * 128 + 128)
+            at = g * per_group * P_SIZE + pair * 128
+            hi, mid, low = split3(
+                jnp.broadcast_to(
+                    pcar[chunks, 0:1, at : at + 128] * factors[0:1, at : at + 128], (16, 128)
+                )
+            )
+            tail = jnp.where(
+                r_iota == 0,
+                hi.astype(F32),
+                jnp.where(
+                    r_iota == 1, mid.astype(F32), jnp.where(r_iota == 2, low.astype(F32), 0.0)
+                ),
+            ).astype(BF16)
+            for half in range(2):
+                q, k = divmod(pair * 2 + half, per_dev)
+                part = slice(half * 64, (half + 1) * 64)
+                send1[g, q, k, 0:64, :] = (
+                    state[g, part, here]
+                    + start_s[g, part, here] * pcar[chunks, 0:1, at : at + 128]
+                ).astype(BF16)
+                send1[g, q, k, 64:80, :] = tail
+
+        def send(s, _):
+            copy1(g, lax.rem(my_q + s, owners)).start()
+            return 0
+
+        if n_ctx > 1:
+            lax.fori_loop(jnp.where(owns(g), 1, 0), owners, send, 0)
+
+        @pl.when(owns(g))
+        def _():
+            recv1[me] = send1[g, my_q]
+
+    def scan_state(g):
+        @pl.when(owns(g))
+        def _():
+            if n_ctx > 1:
+                bulk(recv1.at[pl.ds(0, n_ctx - 1)], ssem1.at[g], rsem1).wait_recv()
+
+            def scan(e, acc):
+                out = []
+                for k in range(per_dev):
+                    send2[e, k] = acc[k].astype(BF16)
+                    got = recv1[e, k].astype(F32)
+                    factor = got[64:65] + got[65:66] + got[66:67]
+                    out.append(acc[k] * factor + got[0:64])
+                return tuple(out)
+
+            lax.fori_loop(
+                0,
+                n_ctx,
+                scan,
+                tuple(jnp.zeros((64, 128), F32) for _ in range(per_dev)),
+                unroll=min(4, n_ctx),
+            )
+
+            def send_back(s, _):
+                copy2(g, lax.rem(me + s, n_ctx)).start()
+                return 0
+
+            lax.fori_loop(1, n_ctx, send_back, 0)
+            recv2[g, my_q] = send2[me]
+
+    def wait_state(g):
+        if n_ctx > 1:
+            if owners > 1:
+
+                @pl.when(owns(g))
+                def _():
+                    bulk(recv2.at[g, pl.ds(0, owners - 1)], ssem2, rsem2.at[g]).wait_recv()
+
+            @pl.when(jnp.logical_not(owns(g)))
+            def _():
+                bulk(recv2.at[g], ssem2, rsem2.at[g]).wait_recv()
+
+    def wait_sends():
+        if n_ctx > 1:
+            for g in range(groups):
+                if owners > 1:
+
+                    @pl.when(owns(g))
+                    def _(g=g):
+                        bulk(send1.at[g, pl.ds(0, owners - 1)], ssem1.at[g], rsem1).wait_send()
+
+                @pl.when(jnp.logical_not(owns(g)))
+                def _(g=g):
+                    bulk(send1.at[g], ssem1.at[g], rsem1).wait_send()
+
+            bulk(send2.at[pl.ds(0, n_ctx - 1)], ssem2, rsem2.at[0]).wait_send()
+
+    lax.fori_loop(1, 6, functools.partial(first, 0, True), 0)
+    pl.semaphore_wait(barrier, n_ctx + n_head - 2)
+    for i in range(3):
+        halo(i).start()
+    lax.fori_loop(6, chunks, functools.partial(first, 0, True), 0)
+    for i in range(3):
+        halo(i).wait_recv()
+    first(0, True, 0, 0)
+    send_state(0)
+    lax.fori_loop(1, chunks, functools.partial(first, 1, False), 0)
+    first(1, False, 0, 0)
+    send_state(1)
+    scan_state(0)
 
     lane = lax.broadcasted_iota(jnp.int32, (L, 128), 1)
 
@@ -369,31 +460,8 @@
         return 0
 
     lax.fori_loop(0, FIRST_PART, second, 0, unroll=4)
-
-    all1.wait_recv()
-
-    def scan(e, acc):
-        out = []
-        for k in range(per_dev):
-            send2[e, k] = acc[k].astype(BF16)
-            got = recv1[e, k].astype(F32)
-            factor = got[64:65] + got[65:66] + got[66:67]
-            out.append(acc[k] * factor + got[0:64])
-        return tuple(out)
-
-    lax.fori_loop(
-        0, n_ctx, scan, tuple(jnp.zeros((64, 128), F32) for _ in range(per_dev)), unroll=4
-    )
-
-    def send_back(s, _):
-        copy2(lax.rem(me + s, n_ctx)).start()
-        return 0
-
-    lax.fori_loop(1, n_ctx, send_back, 0)
-    recv2[me] = send2[me]
+    scan_state(1)
     lax.fori_loop(FIRST_PART, chunks * groups, second, 0, unroll=4)
-
-    all2.wait_recv()
 
     def sum_copy(part, other):
         some = pl.ds(part * 8, 8)
@@ -425,34 +493,33 @@
         sums_recv[my_head, some, :] = sums[some, :]
 
     def add_up(c):
-        total = jnp.sum(squares_s[lax.rem(c, 2)].T, axis=0, keepdims=True)
+        total = jnp.sum(squares_s[c].T, axis=0, keepdims=True)
         sums[pl.ds(c, 1), :] = total
 
-    def third(c, _, w=True, skip_sum=False):
-        if not skip_sum:
-            add_up(c - 1)
+    def enter(g):
+        wide = per_group * P_SIZE
+        for pair in range(wide // 128):
+            here = slice(pair * 128, (pair + 1) * 128)
+            factor = factors[0:1, g * wide + here.start : g * wide + here.stop]
+            for half in range(2):
+                part = slice(half * 64, (half + 1) * 64)
+                k = 2 * pair + half
+                incoming = recv2[g, k // per_dev, k % per_dev].astype(F32)
+                prefix[g, part, here] = incoming
+                start_s[g, part, here] = start_s[g, part, here] + factor * incoming
+
+    def third(g, c, _):
+        i = c * groups + g
         r = pl.ds(pl.multiple_of(c * L, L), L)
-        squares = jnp.zeros((L, 128), F32)
-        for tile in range(x_hbm.shape[1] // TILE):
-            lanes = slice(tile * TILE, (tile + 1) * TILE)
-            g, at = divmod(tile * TILE, per_group * P_SIZE)
+        left = left_s[c]
+        wide = per_group * P_SIZE
+        squares = jnp.zeros((L, 128), F32) if g == 0 else squares_s[c]
+        for at in range(0, wide, TILE):
+            lanes = slice(g * wide + at, g * wide + at + TILE)
             here = slice(at, at + TILE)
-            i = c * groups + g
-            pieces = []
-            for pair in (2 * tile, 2 * tile + 1):
-                pieces.append(
-                    jnp.concatenate(
-                        [
-                            recv2[k // per_dev, k % per_dev].astype(F32)
-                            for k in (2 * pair, 2 * pair + 1)
-                        ],
-                        axis=0,
-                    )
-                )
-            incoming = jnp.concatenate(pieces, axis=1)
-            full = prefix[i, :, here] + pcar[c, 0:1, lanes] * incoming
+            full = prefix[i, :, here] + pcar[c, 0:1, lanes] * start_s[g, :, here]
             inter = dot(cconv[i], full.astype(BF16))
-            spread = dot(left_s[c], sel[1, :, lanes])
+            spread = dot(left, sel[1, :, lanes])
             y = (
                 yint[i, :, here]
                 + spread * inter
@@ -463,19 +530,27 @@
             yint[i, :, here] = gated
             sq = gated * gated
             squares = squares + sq[:, 0:128] + sq[:, 128:256]
-        squares_s[lax.rem(c, 2)] = squares
-        return 0
+        squares_s[c] = squares
+        return 0
+
+    def third_last(c, _):
+        add_up(c - 1)
+        return third(1, c, 0)
 
     gate_copy.wait()
-    third(0, 0, skip_sum=True)
-    lax.fori_loop(1, 9, third, 0)
+    wait_state(0)
+    enter(0)
+    lax.fori_loop(0, chunks, functools.partial(third, 0), 0)
+    wait_state(1)
+    enter(1)
+    third(1, 0, 0)
+    lax.fori_loop(1, 9, third_last, 0)
     send_sums(0)
-    lax.fori_loop(9, chunks, third, 0)
+    lax.fori_loop(9, chunks, third_last, 0)
     add_up(chunks - 1)
     send_sums(1)
 
-    all1.wait_send()
-    all2.wait_send()
+    wait_sends()
     for i in range(3):
         halo(i).wait_send()
 
@@ -531,7 +606,8 @@
         heads = step_size.shape[1]
         groups = b_in.shape[1] // N
         chunks = rows // L
-        per_dev = PIECES // n_ctx
+        owners = max(n_ctx // 2, 1)
+        per_dev = PIECES // owners
         wide = cols // groups
         per_group = heads // groups
         any_spec = pl.BlockSpec(memory_space=pl.ANY)
@@ -544,12 +620,14 @@
             + [pl.BlockSpec(memory_space=pltpu.SMEM)],
             out_specs=vmem,
             scratch_shapes=[
-                pltpu.VMEM((rows + L, cols), BF16),
-                pltpu.VMEM((2, rows + L, groups * N), BF16),
+                pltpu.VMEM((10, L + 16, 128), F32),
+                pltpu.VMEM((rows + RIM, cols), BF16),
+                pltpu.VMEM((2, rows + RIM, groups * N), BF16),
                 pltpu.VMEM((chunks * groups, L, wide), F32),
                 pltpu.VMEM((chunks * groups, L, wide), BF16),
                 pltpu.VMEM((chunks * groups, L, N), BF16),
                 pltpu.VMEM((chunks * groups, N, wide), F32),
+                pltpu.VMEM((groups, N, wide), F32),
                 pltpu.VMEM((groups, N, wide), F32),
                 pltpu.VMEM((chunks + 1, 8, cols), F32),
                 pltpu.VMEM((chunks * heads, L), F32),
@@ -562,11 +640,11 @@
                 pltpu.VMEM((heads, L), F32),
                 pltpu.VMEM((16, cols), F32),
                 pltpu.VMEM((3, L, cols), BF16),
-                pltpu.VMEM((n_ctx, per_dev, ROWS, 128), BF16),
+                pltpu.VMEM((groups, owners, per_dev, ROWS, 128), BF16),
                 pltpu.VMEM((n_ctx, per_dev, ROWS, 128), BF16),
                 pltpu.VMEM((n_ctx, per_dev, 64, 128), BF16),
-                pltpu.VMEM((n_ctx, per_dev, 64, 128), BF16),
-                pltpu.VMEM((2, L, 128), F32),
+                pltpu.VMEM((groups, owners, per_dev, 64, 128), BF16),
+                pltpu.VMEM((chunks, L, 128), F32),
                 pltpu.VMEM((16, L), F32),
                 pltpu.VMEM((n_head, 16, L), F32),
                 pltpu.SemaphoreType.DMA((chunks,)),
@@ -574,10 +652,10 @@
                 pltpu.SemaphoreType.DMA,
                 pltpu.SemaphoreType.DMA((3,)),
                 pltpu.SemaphoreType.DMA((3,)),
+                pltpu.SemaphoreType.DMA((groups,)),
                 pltpu.SemaphoreType.DMA,
                 pltpu.SemaphoreType.DMA,
-                pltpu.SemaphoreType.DMA,
-                pltpu.SemaphoreType.DMA,
+                pltpu.SemaphoreType.DMA((groups,)),
                 pltpu.SemaphoreType.DMA((2,)),
                 pltpu.SemaphoreType.DMA((2,)),
             ],

time: 65.3 us -> 56.9 us (0.87)
  Pallas kernels: 65.1 us -> 56.7 us
    pallas_call x1, Pallas kernels: 62.4 us -> 54 us  [shards(): pl.pallas_call(functools.partial(kernel, n_ctx, n_head, chunks), out_shap...]
where the time goes in v3:
time: 56.9 us; the launch traced here: 56.8 us
  Pallas kernels  56.7 us (100%)
    pallas_call x1, Pallas kernels, shards(): pl.pallas_call(functools.partial(kernel, n_ctx, n_head, chunks), out_shap...  54 us
    pallas_call x1, Pallas kernels, shards(): pl.pallas_call(functools.partial(store, chunks), out_shape=jax.ShapeDtype...  2.75 us

profile of v3, /device:TPU:1, one launch (start us, length us, event | category | flops | bytes accessed | tf_op | source)
XLA Modules:
  0.0 56.8 jit_solution(12631190148197382824)
XLA Ops:
  0.0 54.0 %shard_map.118.from_ref = bf16[1536,2048]{1,0:T(8,128)(2,1)S(1)} custom-call(bf16[1536,2048]{1,0:T(8,128)(2,1)} %x_hbm.1, bf16[1536,256]{1,0:T(8,128)(2,1)} %b_hbm.1, bf16[1536,256]{1,0:T(8,128)(2,1)} %c_hbm.1, bf16[1536,2048]{1,0:T(8,128)(2,1)} %gate_hbm.1, bf16[4,2048]{1,0:T(4,128)(2,1)} %taps_x.1, bf16[4,256]{1,0:T(4,128)(2,1)} %taps_b.1, ...), custom_call_target="tpu_custom_call" | custom-call | tf_op jit(solution)/shard_map/pallas_call | solution.py:615
  54.0 2.8 %shard_map.119 = bf16[1536,2048]{1,0:T(8,128)(2,1)} custom-call(bf16[1536,2048]{1,0:T(8,128)(2,1)S(1)} %shard_map.118.from_ref), custom_call_target="tpu_custom_call" | custom-call | tf_op jit(solution)/shard_map/pallas_call | solution.py:679

commit v4 on v3

--- a/solution.py
+++ b/solution.py
@@ -62,7 +62,6 @@
     xconv,
     cconv,
     prefix,
-    state,
     start_s,
     pcar,
     cum_all,
@@ -74,6 +73,7 @@
     left_s,
     carries,
     factors,
+    skip_s,
     sel,
     send1,
     recv1,
@@ -139,7 +139,7 @@
 
     sel_row = lax.broadcasted_iota(jnp.int32, (L, x_hbm.shape[1]), 0)
     sel_lane = lax.broadcasted_iota(jnp.int32, (L, x_hbm.shape[1]), 1)
-    chosen = jnp.where(lax.rem(sel_row, heads) == lax.div(sel_lane, P_SIZE), 1.0, 0.0)
+    chosen = jnp.where((sel_row & (heads - 1)) == (sel_lane >> 6), 1.0, 0.0)
     sel[0] = jnp.where(sel_row < 2 * heads, chosen, 0.0).astype(BF16)
     sel[1] = jnp.where(sel_row >= 2 * heads, chosen, 0.0).astype(BF16)
     sel[2] = jnp.where(sel_row < 3 * heads, chosen, 0.0).astype(BF16)
@@ -147,10 +147,10 @@
     q_iota = lax.broadcasted_iota(jnp.int32, (L, L), 1)
     pcar[0, 0:1, :] = jnp.zeros((1, pcar.shape[2]), F32)
     pcar[1, 0:1, :] = jnp.ones((1, pcar.shape[2]), F32)
-    state[...] = jnp.zeros_like(state)
     sums[...] = jnp.zeros_like(sums)
     groups = cconv.shape[0] // chunks
     per_group = heads // groups
+    prefix[groups : 2 * groups] = jnp.zeros((groups,) + prefix.shape[1:], F32)
     docs = [doc_ref[d] for d in range(doc_ref.shape[0])]
 
     def seg(pos):
@@ -270,17 +270,17 @@
             parts = []
             for half in range(0, TILE, 128):
                 sub = slice(lanes.start + half, lanes.start + half + 128)
-                x_now = conv(xbuf[window, sub], taps_x[:, sub].astype(F32), keep, 2 + (at + half) // 128).astype(BF16)
-                xconv[i, :, at + half : at + half + 128] = x_now
-                parts.append((x_now.astype(F32) * spread[:, half : half + 128]).astype(BF16))
+                x_now = conv(
+                    xbuf[window, sub], taps_x[:, sub].astype(F32), keep, 2 + (at + half) // 128
+                )
+                xconv[i, :, at + half : at + half + 128] = x_now.astype(BF16)
+                parts.append((x_now * spread[:, half : half + 128]).astype(BF16))
             local = dot(b_t, jnp.concatenate(parts, axis=1))
             if at_start:
                 start_s[g, :, here] = local
                 continue
             factor = factors[pl.ds(c, 1), lanes]
-            before = state[g, :, here]
-            prefix[i, :, here] = before
-            state[g, :, here] = before * factor + local
+            prefix[i + groups, :, here] = prefix[i, :, here] * factor + local
             pcar[c + 1, 0:1, lanes] = pcar[c, 0:1, lanes] * factor
         return 0
 
@@ -352,7 +352,7 @@
                 q, k = divmod(pair * 2 + half, per_dev)
                 part = slice(half * 64, (half + 1) * 64)
                 send1[g, q, k, 0:64, :] = (
-                    state[g, part, here]
+                    prefix[chunks * groups + g, part, here]
                     + start_s[g, part, here] * pcar[chunks, 0:1, at : at + 128]
                 ).astype(BF16)
                 send1[g, q, k, 64:80, :] = tail
@@ -425,20 +425,23 @@
 
             bulk(send2.at[pl.ds(0, n_ctx - 1)], ssem2, rsem2.at[0]).wait_send()
 
-    lax.fori_loop(1, 6, functools.partial(first, 0, True), 0)
+    lax.fori_loop(1, 6, functools.partial(first, 0, True), 0, unroll=2)
     pl.semaphore_wait(barrier, n_ctx + n_head - 2)
     for i in range(3):
         halo(i).start()
-    lax.fori_loop(6, chunks, functools.partial(first, 0, True), 0)
+    lax.fori_loop(6, chunks, functools.partial(first, 0, True), 0, unroll=2)
     for i in range(3):
         halo(i).wait_recv()
     first(0, True, 0, 0)
     send_state(0)
-    lax.fori_loop(1, chunks, functools.partial(first, 1, False), 0)
+    lax.fori_loop(1, chunks, functools.partial(first, 1, False), 0, unroll=2)
     first(1, False, 0, 0)
     send_state(1)
     scan_state(0)
 
+    wide = per_group * P_SIZE
+    for g in range(groups):
+        skip_s[g, 0:1, :] = factors[chunks : chunks + 1, g * wide : (g + 1) * wide]
     lane = lax.broadcasted_iota(jnp.int32, (L, 128), 1)
 
     def second(i, _):
@@ -456,12 +459,16 @@
                 [jnp.where(lane < P_SIZE, x_pair, zero), jnp.where(lane < P_SIZE, zero, x_pair)],
                 axis=0,
             )
-            yint[i, :, pair * 128 : (pair + 1) * 128] = dot(jnp.concatenate(ws, axis=1), both)
-        return 0
-
-    lax.fori_loop(0, FIRST_PART, second, 0, unroll=4)
+            here = slice(pair * 128, (pair + 1) * 128)
+            yint[i, :, here] = (
+                dot(jnp.concatenate(ws, axis=1), both)
+                + skip_s[lax.rem(i, groups), 0:1, here] * x_pair.astype(F32)
+            )
+        return 0
+
+    lax.fori_loop(0, FIRST_PART, second, 0, unroll=6)
     scan_state(1)
-    lax.fori_loop(FIRST_PART, chunks * groups, second, 0, unroll=4)
+    lax.fori_loop(FIRST_PART, chunks * groups, second, 0, unroll=6)
 
     def sum_copy(part, other):
         some = pl.ds(part * 8, 8)
@@ -492,9 +499,12 @@
         some = slice(part * 8, part * 8 + 8)
         sums_recv[my_head, some, :] = sums[some, :]
 
+    def sum_row(c):
+        return jnp.where(c >= chunks - 2, c + 6, c)
+
     def add_up(c):
         total = jnp.sum(squares_s[c].T, axis=0, keepdims=True)
-        sums[pl.ds(c, 1), :] = total
+        sums[pl.ds(sum_row(c), 1), :] = total
 
     def enter(g):
         wide = per_group * P_SIZE
@@ -520,11 +530,7 @@
             full = prefix[i, :, here] + pcar[c, 0:1, lanes] * start_s[g, :, here]
             inter = dot(cconv[i], full.astype(BF16))
             spread = dot(left, sel[1, :, lanes])
-            y = (
-                yint[i, :, here]
-                + spread * inter
-                + factors[chunks : chunks + 1, lanes] * xconv[i, :, here].astype(F32)
-            )
+            y = yint[i, :, here] + spread * inter
             v = gate_buf[r, lanes].astype(F32) * 0.5
             gated = y * (v + v * jnp.tanh(v))
             yint[i, :, here] = gated
@@ -540,15 +546,17 @@
     gate_copy.wait()
     wait_state(0)
     enter(0)
-    lax.fori_loop(0, chunks, functools.partial(third, 0), 0)
+    lax.fori_loop(0, chunks, functools.partial(third, 0), 0, unroll=2)
     wait_state(1)
     enter(1)
     third(1, 0, 0)
     lax.fori_loop(1, 9, third_last, 0)
     send_sums(0)
-    lax.fori_loop(9, chunks, third_last, 0)
+    lax.fori_loop(9, chunks - 1, third_last, 0)
+    send_sums(1)
+    third_last(chunks - 1, 0)
     add_up(chunks - 1)
-    send_sums(1)
+    send_sums(2)
 
     wait_sends()
     for i in range(3):
@@ -557,9 +565,10 @@
     columns = n_head * heads * P_SIZE
 
     def norm(c, _):
-        total = sums_recv[0, pl.ds(c, 1), :]
+        at_row = sum_row(c)
+        total = sums_recv[0, pl.ds(at_row, 1), :]
         for k in range(1, n_head):
-            total = total + sums_recv[k, pl.ds(c, 1), :]
+            total = total + sums_recv[k, pl.ds(at_row, 1), :]
         row = lax.rsqrt(total / columns + EPS)
         scale = jnp.broadcast_to(row, (L, L)).T
         r = pl.ds(pl.multiple_of(c * L, L), L)
@@ -573,9 +582,11 @@
     sums_in(0).wait_recv()
     lax.fori_loop(0, 8, norm, 0)
     sums_in(1).wait_recv()
-    lax.fori_loop(8, chunks, norm, 0)
-    sums_in(0).wait_send()
-    sums_in(1).wait_send()
+    lax.fori_loop(8, chunks - 2, norm, 0)
+    sums_in(2).wait_recv()
+    lax.fori_loop(chunks - 2, chunks, norm, 0)
+    for part in range(3):
+        sums_in(part).wait_send()
 
 
 def store(chunks, from_ref, out_hbm, sem):
@@ -626,8 +637,7 @@
                 pltpu.VMEM((chunks * groups, L, wide), F32),
                 pltpu.VMEM((chunks * groups, L, wide), BF16),
                 pltpu.VMEM((chunks * groups, L, N), BF16),
-                pltpu.VMEM((chunks * groups, N, wide), F32),
-                pltpu.VMEM((groups, N, wide), F32),
+                pltpu.VMEM(((chunks + 1) * groups, N, wide), F32),
                 pltpu.VMEM((groups, N, wide), F32),
                 pltpu.VMEM((chunks + 1, 8, cols), F32),
                 pltpu.VMEM((chunks * heads, L), F32),
@@ -639,14 +649,15 @@
                 pltpu.VMEM((chunks, L, L), BF16),
                 pltpu.VMEM((heads, L), F32),
                 pltpu.VMEM((16, cols), F32),
+                pltpu.VMEM((groups, 8, wide), F32),
                 pltpu.VMEM((3, L, cols), BF16),
                 pltpu.VMEM((groups, owners, per_dev, ROWS, 128), BF16),
                 pltpu.VMEM((n_ctx, per_dev, ROWS, 128), BF16),
                 pltpu.VMEM((n_ctx, per_dev, 64, 128), BF16),
                 pltpu.VMEM((groups, owners, per_dev, 64, 128), BF16),
                 pltpu.VMEM((chunks, L, 128), F32),
-                pltpu.VMEM((16, L), F32),
-                pltpu.VMEM((n_head, 16, L), F32),
+                pltpu.VMEM((24, L), F32),
+                pltpu.VMEM((n_head, 24, L), F32),
                 pltpu.SemaphoreType.DMA((chunks,)),
                 pltpu.SemaphoreType.DMA((2,)),
                 pltpu.SemaphoreType.DMA,
@@ -656,11 +667,11 @@
                 pltpu.SemaphoreType.DMA,
                 pltpu.SemaphoreType.DMA,
                 pltpu.SemaphoreType.DMA((groups,)),
-                pltpu.SemaphoreType.DMA((2,)),
-                pltpu.SemaphoreType.DMA((2,)),
+                pltpu.SemaphoreType.DMA((3,)),
+                pltpu.SemaphoreType.DMA((3,)),
             ],
             compiler_params=pltpu.CompilerParams(
-                collective_id=0, has_side_effects=True, vmem_limit_bytes=56 * 1024 * 1024
+                collective_id=0, has_side_effects=True, vmem_limit_bytes=57 * 1024 * 1024 + 512 * 1024
             ),
         )(
             x_in,

time: 56.9 us -> 54.7 us (0.961)
  Pallas kernels: 56.7 us -> 54.6 us
    pallas_call x1, Pallas kernels: 54 us -> 51.9 us  [shards(): pl.pallas_call(functools.partial(kernel, n_ctx, n_head, chunks), out_shap...]
where the time goes in v4:
time: 54.7 us; the launch traced here: 54.6 us
  Pallas kernels  54.6 us (100%)
    pallas_call x1, Pallas kernels, shards(): pl.pallas_call(functools.partial(kernel, n_ctx, n_head, chunks), out_shap...  51.9 us
    pallas_call x1, Pallas kernels, shards(): pl.pallas_call(functools.partial(store, chunks), out_shape=jax.ShapeDtype...  2.75 us

profile of v4, /device:TPU:1, one launch (start us, length us, event | category | flops | bytes accessed | tf_op | source)
XLA Modules:
  0.0 54.6 jit_solution(8986936698387486153)
XLA Ops:
  0.0 51.9 %shard_map.118.from_ref = bf16[1536,2048]{1,0:T(8,128)(2,1)S(1)} custom-call(bf16[1536,2048]{1,0:T(8,128)(2,1)} %x_hbm.1, bf16[1536,256]{1,0:T(8,128)(2,1)} %b_hbm.1, bf16[1536,256]{1,0:T(8,128)(2,1)} %c_hbm.1, bf16[1536,2048]{1,0:T(8,128)(2,1)} %gate_hbm.1, bf16[4,2048]{1,0:T(4,128)(2,1)} %taps_x.1, bf16[4,256]{1,0:T(4,128)(2,1)} %taps_b.1, ...), custom_call_target="tpu_custom_call" | custom-call | tf_op jit(solution)/shard_map/pallas_call | solution.py:626
  51.9 2.8 %shard_map.119 = bf16[1536,2048]{1,0:T(8,128)(2,1)} custom-call(bf16[1536,2048]{1,0:T(8,128)(2,1)S(1)} %shard_map.118.from_ref), custom_call_target="tpu_custom_call" | custom-call | tf_op jit(solution)/shard_map/pallas_call | solution.py:690

commit v5 on v4

--- a/solution.py
+++ b/solution.py
@@ -16,7 +16,6 @@
 RIM = 16
 L = 128
 TILE = 256
-CONV_TILE = 128
 EPS = 1e-05
 LOG2E = math.log2(math.e)
 HI = lax.Precision.HIGHEST
@@ -69,7 +68,6 @@
     cumt_s,
     allow_s,
     scores_s,
-    keep_s,
     left_s,
     carries,
     factors,
@@ -79,7 +77,6 @@
     recv1,
     send2,
     recv2,
-    squares_s,
     sums,
     sums_recv,
     x_sem,
@@ -208,7 +205,7 @@
             gap = base + t_iota - d
             since = jnp.minimum(since, jnp.where(gap < 0, 4, gap))
         for s in range(1, K):
-            keep_s[c, s - 1] = jnp.where(since < s, 0.0, 1.0)
+            yint[c, :, (s - 1) * L : s * L] = jnp.where(since < s, 0.0, 1.0)
         return 0
 
     lax.fori_loop(0, chunks, decays, 0, unroll=4)
@@ -254,7 +251,7 @@
             x_copy(c).wait()
         i = c * groups + g
         window = pl.ds(pl.multiple_of(c * L, L), L + RIM)
-        keep = [keep_s[c, s] for s in range(K - 1)]
+        keep = [yint[c, :, s * L : (s + 1) * L] for s in range(K - 1)]
         left = left_s[c]
         mine = slice(g * N, (g + 1) * N)
         b_now = conv(bcbuf[0, window, mine], taps_b[:, mine].astype(F32), keep, 0)
@@ -503,7 +500,7 @@
         return jnp.where(c >= chunks - 2, c + 6, c)
 
     def add_up(c):
-        total = jnp.sum(squares_s[c].T, axis=0, keepdims=True)
+        total = jnp.sum(allow_s[c].T, axis=0, keepdims=True)
         sums[pl.ds(sum_row(c), 1), :] = total
 
     def enter(g):
@@ -523,7 +520,7 @@
         r = pl.ds(pl.multiple_of(c * L, L), L)
         left = left_s[c]
         wide = per_group * P_SIZE
-        squares = jnp.zeros((L, 128), F32) if g == 0 else squares_s[c]
+        squares = jnp.zeros((L, 128), F32) if g == 0 else allow_s[c]
         for at in range(0, wide, TILE):
             lanes = slice(g * wide + at, g * wide + at + TILE)
             here = slice(at, at + TILE)
@@ -536,7 +533,7 @@
             yint[i, :, here] = gated
             sq = gated * gated
             squares = squares + sq[:, 0:128] + sq[:, 128:256]
-        squares_s[c] = squares
+        allow_s[c] = squares
         return 0
 
     def third_last(c, _):
@@ -550,9 +547,9 @@
     wait_state(1)
     enter(1)
     third(1, 0, 0)
-    lax.fori_loop(1, 9, third_last, 0)
+    lax.fori_loop(1, 9, third_last, 0, unroll=2)
     send_sums(0)
-    lax.fori_loop(9, chunks - 1, third_last, 0)
+    lax.fori_loop(9, chunks - 1, third_last, 0, unroll=2)
     send_sums(1)
     third_last(chunks - 1, 0)
     add_up(chunks - 1)
@@ -580,11 +577,11 @@
         return 0
 
     sums_in(0).wait_recv()
-    lax.fori_loop(0, 8, norm, 0)
+    lax.fori_loop(0, 8, norm, 0, unroll=2)
     sums_in(1).wait_recv()
-    lax.fori_loop(8, chunks - 2, norm, 0)
+    lax.fori_loop(8, chunks - 2, norm, 0, unroll=2)
     sums_in(2).wait_recv()
-    lax.fori_loop(chunks - 2, chunks, norm, 0)
+    lax.fori_loop(chunks - 2, chunks, norm, 0, unroll=2)
     for part in range(3):
         sums_in(part).wait_send()
 
@@ -645,7 +642,6 @@
                 pltpu.VMEM((chunks * groups, per_group, L), F32),
                 pltpu.VMEM((chunks, L, L), F32),
                 pltpu.VMEM((chunks * groups, L, L), F32),
-                pltpu.VMEM((chunks, K - 1, L, L), F32),
                 pltpu.VMEM((chunks, L, L), BF16),
                 pltpu.VMEM((heads, L), F32),
                 pltpu.VMEM((16, cols), F32),
@@ -655,7 +651,6 @@
                 pltpu.VMEM((n_ctx, per_dev, ROWS, 128), BF16),
                 pltpu.VMEM((n_ctx, per_dev, 64, 128), BF16),
                 pltpu.VMEM((groups, owners, per_dev, 64, 128), BF16),
-                pltpu.VMEM((chunks, L, 128), F32),
                 pltpu.VMEM((24, L), F32),
                 pltpu.VMEM((n_head, 24, L), F32),
                 pltpu.SemaphoreType.DMA((chunks,)),

time: 54.7 us -> 54.4 us (level)
  no operation moved by 1% of the time
where the time goes in v5:
time: 54.4 us; the launch traced here: 54.3 us
  Pallas kernels  54.1 us (99%)
    pallas_call x1, Pallas kernels, shards(): pl.pallas_call(functools.partial(kernel, n_ctx, n_head, chunks), out_shap...  51.4 us
    pallas_call x1, Pallas kernels, shards(): pl.pallas_call(functools.partial(store, chunks), out_shape=jax.ShapeDtype...  2.75 us

profile of v5, /device:TPU:1, one launch (start us, length us, event | category | flops | bytes accessed | tf_op | source)
XLA Modules:
  0.0 54.3 jit_solution(3575295239925101926)
XLA Ops:
  0.0 51.4 %shard_map.118.from_ref = bf16[1536,2048]{1,0:T(8,128)(2,1)S(1)} custom-call(bf16[1536,2048]{1,0:T(8,128)(2,1)} %x_hbm.1, bf16[1536,256]{1,0:T(8,128)(2,1)} %b_hbm.1, bf16[1536,256]{1,0:T(8,128)(2,1)} %c_hbm.1, bf16[1536,2048]{1,0:T(8,128)(2,1)} %gate_hbm.1, bf16[4,2048]{1,0:T(4,128)(2,1)} %taps_x.1, bf16[4,256]{1,0:T(4,128)(2,1)} %taps_b.1, ...), custom_call_target="tpu_custom_call" | custom-call | tf_op jit(solution)/shard_map/pallas_call | solution.py:623
  51.4 2.8 %shard_map.119 = bf16[1536,2048]{1,0:T(8,128)(2,1)} custom-call(bf16[1536,2048]{1,0:T(8,128)(2,1)S(1)} %shard_map.118.from_ref), custom_call_target="tpu_custom_call" | custom-call | tf_op jit(solution)/shard_map/pallas_call | solution.py:685
